TPU v7x, 256 devices: a whole 4x4x8 slice. The times are simulated.
256 devices in a mesh: gx: 16 (over y, z_hi), gy: 4 (over x), gz: 4 (over z_lo, core).
Axes of the slice: x: 4, y: 4, z: 8 (z_hi: 4, z_lo: 2; z = z_hi * 2 + z_lo), core: 2. Of those that a mesh axis runs over, the one named last changes fastest.
Arguments:
- fine: bfloat16 [256, 128, 32, 128], P('gx', 'gy', 'gz'), may hold values from -6 to 6
- occupied: int32 [16, 8, 4], P('gx', 'gy', 'gz'), may hold values 0 or 1
- w_down: bfloat16 [4, 128, 128], replicated, may hold values from -0.25 to 0.25
- w_conv: bfloat16 [27, 128, 128], replicated, may hold values from -0.109375 to 0.109375
- cotangent: bfloat16 [128, 64, 32, 128], P('gx', 'gy', 'gz'), may hold values from -6 to 6
Outputs:
- section_out: bfloat16 [128, 64, 32, 128], P('gx', 'gy', 'gz')
- d_fine: bfloat16 [256, 128, 32, 128], P('gx', 'gy', 'gz')
- d_wconv: float32 [27, 128, 128], P(None, 'gx')
- d_wdown: float32 [4, 128, 128], P(None, 'gx')
All inputs are finite; a program needn't handle non-finite values. No bound on the sum of `occupied` on one device may be relied on, other than what follows from the above.
Results may differ from a plain program's by a relative error of at most 0.013.
Values may be sent and summed in bfloat16 or wider, within the bound.
A program may use at most 64 MiB of HBM per device.

v0:
```python
import jax
import jax.numpy as jnp
from jax import lax
from jax.sharding import PartitionSpec as P

BRICK = 8


def padded(block, sides, width):
    for axis, dim in sides:
        count = lax.axis_size(axis)
        forward = [(i, i + 1) for i in range(count - 1)]
        backward = [(target, source) for source, target in forward]
        low = lax.ppermute(
            lax.slice_in_dim(block, block.shape[dim] - width, None, axis=dim), axis, forward
        )
        high = lax.ppermute(lax.slice_in_dim(block, 0, width, axis=dim), axis, backward)
        block = jnp.concatenate([low, block, high], axis=dim)
    return block


def expand_mask(occupied):
    cells = occupied.astype(jnp.float32)
    cells = jnp.repeat(cells, BRICK, axis=0)
    cells = jnp.repeat(cells, BRICK, axis=1)
    cells = jnp.repeat(cells, BRICK, axis=2)
    return cells[..., None]


def patches(fine):
    sizex = fine.shape[0] // 2
    sizey = fine.shape[1] // 2
    split = fine.reshape(sizex, 2, sizey, 2, fine.shape[2], fine.shape[3])
    return [split[:, a, :, b] for a in range(2) for b in range(2)]


def section_block(act_pad, grad_pad, w_conv, sizex, sizey, sizez):
    width = w_conv.shape[1]
    cells = sizex * sizey * sizez
    masked_flat = grad_pad[1 : 1 + sizex, 1 : 1 + sizey, 1 : 1 + sizez].reshape(cells, width)
    forward = jnp.zeros((cells, width), jnp.float32)
    backward = jnp.zeros((cells, width), jnp.float32)
    grads = []
    for dx in range(3):
        for dy in range(3):
            for dz in range(3):
                tap = 9 * dx + 3 * dy + dz
                ahead = act_pad[dx : dx + sizex, dy : dy + sizey, dz : dz + sizez].reshape(
                    cells, width
                )
                behind = grad_pad[
                    2 - dx : 2 - dx + sizex, 2 - dy : 2 - dy + sizey, 2 - dz : 2 - dz + sizez
                ].reshape(cells, width)
                forward = forward + jnp.dot(ahead, w_conv[tap], preferred_element_type=jnp.float32)
                backward = backward + lax.dot_general(
                    behind,
                    w_conv[tap],
                    (((1,), (1,)), ((), ())),
                    preferred_element_type=jnp.float32,
                )
                grads.append(
                    lax.dot_general(
                        ahead,
                        masked_flat,
                        (((0,), (0,)), ((), ())),
                        preferred_element_type=jnp.float32,
                    )
                )
    return (
        forward.reshape(sizex, sizey, sizez, width),
        backward.reshape(sizex, sizey, sizez, width),
        jnp.stack(grads),
    )


def body(fine, occupied, w_down, w_conv, cotangent):
    occ = expand_mask(occupied)
    sizex, sizey, sizez, width = cotangent.shape
    cells = sizex * sizey * sizez
    pieces = patches(fine)
    down = jnp.zeros((cells, width), jnp.float32)
    for index in range(4):
        down = down + jnp.dot(
            pieces[index].reshape(cells, -1), w_down[index], preferred_element_type=jnp.float32
        )
    z_val = (occ * down.reshape(sizex, sizey, sizez, width)).astype(jnp.bfloat16)
    act = jnp.maximum(z_val, jnp.zeros((), jnp.bfloat16))
    masked = (occ * cotangent.astype(jnp.float32)).astype(jnp.bfloat16)
    act_pad = padded(act, (("gx", 0), ("gy", 1), ("gz", 2)), 1)
    grad_pad = padded(masked, (("gx", 0), ("gy", 1), ("gz", 2)), 1)
    forward, backward, grads = section_block(act_pad, grad_pad, w_conv, sizex, sizey, sizez)
    total_cells = cells * lax.axis_size("gx") * lax.axis_size("gy") * lax.axis_size("gz")
    scale = float(total_cells) ** (-0.5)
    section_out = (z_val.astype(jnp.float32) + occ * forward).astype(jnp.bfloat16)
    positive = z_val > 0
    dz_val = (occ * (cotangent.astype(jnp.float32) + jnp.where(positive, backward, 0.0))).astype(
        jnp.bfloat16
    )
    dz_flat = dz_val.reshape(cells, width)
    down_grads = []
    outputs = []
    for index in range(4):
        down_grads.append(
            lax.dot_general(
                pieces[index].reshape(cells, -1),
                dz_flat,
                (((0,), (0,)), ((), ())),
                preferred_element_type=jnp.float32,
            )
        )
        outputs.append(
            lax.dot_general(
                dz_flat, w_down[index], (((1,), (1,)), ((), ())), preferred_element_type=jnp.float32
            ).astype(jnp.bfloat16)
        )
    conv_terms = grads * scale
    down_terms = jnp.stack(down_grads) * scale
    whole_conv, whole_down = lax.psum((conv_terms, down_terms), ("gy", "gz"))
    d_wconv, d_wdown = (
        lax.psum_scatter(whole_conv, "gx", scatter_dimension=1, tiled=True),
        lax.psum_scatter(whole_down, "gx", scatter_dimension=1, tiled=True),
    )
    stacked = jnp.stack(outputs).reshape(2, 2, sizex, sizey, sizez, -1)
    d_fine = jnp.transpose(stacked, (2, 0, 3, 1, 4, 5)).reshape(2 * sizex, 2 * sizey, sizez, -1)
    return (section_out, d_fine, d_wconv, d_wdown)


def solution(mesh):
    in_specs = (P("gx", "gy", "gz", None), P("gx", "gy", "gz"), P(), P(), P("gx", "gy", "gz", None))
    out_specs = (
        P("gx", "gy", "gz", None),
        P("gx", "gy", "gz", None),
        P(None, "gx", None),
        P(None, "gx", None),
    )
    return jax.shard_map(body, mesh=mesh, in_specs=in_specs, out_specs=out_specs, check_vma=False)
```

profile of v0, /device:TPU:1, one launch (start us, length us, event | category | flops | bytes accessed | tf_op | source)
XLA Modules:
  0.0 467.5 jit_solution(13598448727872504769)
XLA Ops:
  9.2 5.7 %collective-permute-start.6 = (bf16[1,16,8,128]{3,1,2,0:T(8,128)(2,1)S(1)}, bf16[1,16,8,128]{3,1,2,0:T(8,128)(2,1)S(1)}, u32[]{:S(2)}, u32[]{:S(2)}) collective-permute-start(bf16[1,16,8,128]{3,1,2,0:T(8,128)(2,1)S(1)} %get-tuple-element.92), channel_id=1, source_target_pairs={{0,16},{16,32},{32,48},{48,64},{64,80},{80,96},{96,112},{112,128},... | collective-permute-start | bytes 98312 | tf_op jit(solution)/shard_map/ppermute | solution.py:14
  14.9 1.3 collective-permute-start.7
  16.2 1.3 fusion.202
  18.6 3.7 collective-permute-done.7
  22.4 3.1 collective-permute-start.8
  25.5 1.3 collective-permute-start.9
  27.0 3.2 collective-permute-done.9
  30.3 5.2 %collective-permute-start.10 = (bf16[10,18,1,128]{3,1,2,0:T(8,128)(2,1)S(1)}, bf16[10,18,1,128]{3,1,2,0:T(8,128)(2,1)S(1)}, u32[]{:S(2)}, u32[]{:S(2)}) collective-permute-start(bf16[10,18,1,128]{3,1,2,0:T(8,128)(2,1)S(1)} %get-tuple-element.77), channel_id=1, source_target_pairs={{1,0},{2,1},{3,2},{5,4},{6,5},{7,6},{9,8},{10,9},{11,10},{13,12},{... | collective-permute-start | bytes 138248 | tf_op jit(solution)/shard_map/ppermute | solution.py:17
  35.5 2.5 collective-permute-start.11
  50.5 5.7 %collective-permute-start = (bf16[1,16,8,128]{3,1,2,0:T(8,128)(2,1)S(1)}, bf16[1,16,8,128]{3,1,2,0:T(8,128)(2,1)S(1)}, u32[]{:S(2)}, u32[]{:S(2)}) collective-permute-start(bf16[1,16,8,128]{3,1,2,0:T(8,128)(2,1)S(1)} %get-tuple-element.88), channel_id=1, source_target_pairs={{0,16},{16,32},{32,48},{48,64},{64,80},{80,96},{96,112},{112,128},... | collective-permute-start | bytes 98312 | tf_op jit(solution)/shard_map/ppermute | solution.py:14
  56.2 1.3 collective-permute-start.1
  57.6 4.6 collective-permute-done.1
  62.3 3.1 collective-permute-start.2
  66.7 3.4 collective-permute-done.3
  70.2 6.7 %collective-permute-start.4 = (bf16[10,18,1,128]{3,1,2,0:T(8,128)(2,1)S(1)}, bf16[10,18,1,128]{3,1,2,0:T(8,128)(2,1)S(1)}, u32[]{:S(2)}, u32[]{:S(2)}) collective-permute-start(bf16[10,18,1,128]{3,1,2,0:T(8,128)(2,1)S(1)} %get-tuple-element.73), channel_id=1, source_target_pairs={{0,1},{1,2},{2,3},{4,5},{5,6},{6,7},{8,9},{9,10},{10,11},{12,13},{... | collective-permute-start | bytes 138248 | tf_op jit(solution)/shard_map/ppermute | solution.py:14
  76.9 2.1 collective-permute-start.5
  79.4 3.1 collective-permute-done.5
  90.5 1.4 broadcast_multiply_fusion
  100.5 1.8 copy.136
  119.2 55.9 %reduce-scatter.2.cloned.1.call-done = f32[27,8,128]{2,1,0:T(8,128)} async-done(((f32[27,128,128]{2,1,0:T(8,128)}), f32[27,8,128]{2,1,0:T(8,128)}) %reduce-scatter.2.cloned.1.call-update) | async-done | bytes 110608 | tf_op jit(solution)/shard_map/reduce_scatter | solution.py:120
  175.1 157.2 %all-reduce.6.cloned.1.call-done = f32[4,128,128]{2,0,1:T(4,128)} async-done(((f32[4,128,128]{2,0,1:T(4,128)}), f32[4,128,128]{2,0,1:T(4,128)}) %all-reduce.6.cloned.1.call-update) | async-done | bytes 262160
  333.1 59.6 %psum.17 = f32[4,8,128]{2,0,1:T(4,128)S(1)} all-reduce(f32[4,8,128]{2,0,1:T(4,128)S(1)} %constant_dynamic-slice_fusion), channel_id=1, replica_groups=mesh['gx'=16,'gy'=4,'gz'=4] {'gy','gz'}, use_global_device_ids=true, to_apply=%region_2.3 | all-reduce | flops 4096 | bytes 32768 | tf_op jit(solution)/shard_map/psum | solution.py:118
  393.3 66.1 %all-reduce.4.cloned.1.call-done = f32[27,8,128]{2,1,0:T(8,128)} async-done(((f32[27,8,128]{2,1,0:T(8,128)}), f32[27,8,128]{2,1,0:T(8,128)}) %all-reduce.4.cloned.1.call-update) | async-done | bytes 110608 | tf_op jit(solution)/shard_map/psum | solution.py:118
  459.4 1.5 copy.208
  (223 shorter events, 50.5 us)
Async XLA Ops:
  7.2 10.4 %copy-start.12 = (bf16[4,128,128]{2,1,0:T(8,128)(2,1)S(1)}, bf16[4,128,128]{2,1,0:T(8,128)(2,1)}, u32[]{:S(2)}) copy-start(bf16[4,128,128]{2,1,0:T(8,128)(2,1)} %param.7) | copy-start | bytes 393220
  7.2 167.9 %reduce-scatter.2.cloned.1.call-start = ((), (), s32[]{:S(2)}) async-start(), calls=%async_computation.1 | async-start | bytes 1880064 | tf_op jit(solution)/shard_map/reduce_scatter | solution.py:120
  9.2 9.5 %collective-permute-start.6 = (bf16[1,16,8,128]{3,1,2,0:T(8,128)(2,1)S(1)}, bf16[1,16,8,128]{3,1,2,0:T(8,128)(2,1)S(1)}, u32[]{:S(2)}, u32[]{:S(2)}) collective-permute-start(bf16[1,16,8,128]{3,1,2,0:T(8,128)(2,1)S(1)} %get-tuple-element.92), channel_id=1, source_target_pairs={{0,16},{16,32},{32,48},{48,64},{64,80},{80,96},{96,112},{112,128},... | collective-permute-start | bytes 98312 | tf_op jit(solution)/shard_map/ppermute | solution.py:14
  14.9 7.4 %collective-permute-start.7 = (bf16[1,16,8,128]{3,1,2,0:T(8,128)(2,1)S(1)}, bf16[1,16,8,128]{3,1,2,0:T(8,128)(2,1)S(1)}, u32[]{:S(2)}, u32[]{:S(2)}) collective-permute-start(bf16[1,16,8,128]{3,1,2,0:T(8,128)(2,1)S(1)} %get-tuple-element.93), channel_id=1, source_target_pairs={{16,0},{32,16},{48,32},{64,48},{80,64},{96,80},{112,96},{128,112},... | collective-permute-start | bytes 98312 | tf_op jit(solution)/shard_map/ppermute | solution.py:17
  17.5 1.0 copy-start.7
  17.5 1.0 copy-start.8
  22.4 4.6 collective-permute-start.8
  25.5 4.7 %collective-permute-start.9 = (bf16[10,1,8,128]{3,1,2,0:T(2,128)(2,1)S(1)}, bf16[10,1,8,128]{3,1,2,0:T(2,128)(2,1)S(1)}, u32[]{:S(2)}, u32[]{:S(2)}) collective-permute-start(bf16[10,1,8,128]{3,1,2,0:T(2,128)(2,1)S(1)} %get-tuple-element.85), channel_id=1, source_target_pairs={{4,0},{8,4},{12,8},{5,1},{9,5},{13,9},{6,2},{10,6},{14,10},{7,3},{... | collective-permute-start | bytes 61448 | tf_op jit(solution)/shard_map/ppermute | solution.py:17
  30.3 8.8 %collective-permute-start.10 = (bf16[10,18,1,128]{3,1,2,0:T(8,128)(2,1)S(1)}, bf16[10,18,1,128]{3,1,2,0:T(8,128)(2,1)S(1)}, u32[]{:S(2)}, u32[]{:S(2)}) collective-permute-start(bf16[10,18,1,128]{3,1,2,0:T(8,128)(2,1)S(1)} %get-tuple-element.77), channel_id=1, source_target_pairs={{1,0},{2,1},{3,2},{5,4},{6,5},{7,6},{9,8},{10,9},{11,10},{13,12},{... | collective-permute-start | bytes 138248 | tf_op jit(solution)/shard_map/ppermute | solution.py:17
  35.5 3.8 collective-permute-start.11
  41.6 1.2 copy-start
  50.4 36.1 %copy-start.4 = (bf16[8,16,8,128]{3,1,2,0:T(8,128)(2,1)}, bf16[8,16,8,128]{3,1,2,0:T(8,128)(2,1)S(1)}, u32[]{:S(2)}) copy-start(bf16[8,16,8,128]{3,1,2,0:T(8,128)(2,1)S(1)} %get-tuple-element.17) | copy-start | bytes 786436
  50.5 7.1 %collective-permute-start = (bf16[1,16,8,128]{3,1,2,0:T(8,128)(2,1)S(1)}, bf16[1,16,8,128]{3,1,2,0:T(8,128)(2,1)S(1)}, u32[]{:S(2)}, u32[]{:S(2)}) collective-permute-start(bf16[1,16,8,128]{3,1,2,0:T(8,128)(2,1)S(1)} %get-tuple-element.88), channel_id=1, source_target_pairs={{0,16},{16,32},{32,48},{48,64},{64,80},{80,96},{96,112},{112,128},... | collective-permute-start | bytes 98312 | tf_op jit(solution)/shard_map/ppermute | solution.py:14
  56.2 6.0 %collective-permute-start.1 = (bf16[1,16,8,128]{3,1,2,0:T(8,128)(2,1)S(1)}, bf16[1,16,8,128]{3,1,2,0:T(8,128)(2,1)S(1)}, u32[]{:S(2)}, u32[]{:S(2)}) collective-permute-start(bf16[1,16,8,128]{3,1,2,0:T(8,128)(2,1)S(1)} %get-tuple-element.89), channel_id=1, source_target_pairs={{16,0},{32,16},{48,32},{64,48},{80,64},{96,80},{112,96},{128,112},... | collective-permute-start | bytes 98312 | tf_op jit(solution)/shard_map/ppermute | solution.py:17
  57.5 26.5 %copy-start.10 = (bf16[1,16,8,128]{3,1,2,0:T(8,128)(2,1)}, bf16[1,16,8,128]{3,1,2,0:T(8,128)(2,1)S(1)}, u32[]{:S(2)}) copy-start(bf16[1,16,8,128]{3,1,2,0:T(8,128)(2,1)S(1)} %collective-permute-done) | copy-start | bytes 98308
  62.2 26.9 %copy-start.11 = (bf16[1,16,8,128]{3,1,2,0:T(8,128)(2,1)}, bf16[1,16,8,128]{3,1,2,0:T(8,128)(2,1)S(1)}, u32[]{:S(2)}) copy-start(bf16[1,16,8,128]{3,1,2,0:T(8,128)(2,1)S(1)} %collective-permute-done.1) | copy-start | bytes 98308
  62.3 4.4 collective-permute-start.2
  65.4 4.7 %collective-permute-start.3 = (bf16[10,1,8,128]{3,1,2,0:T(2,128)(2,1)S(1)}, bf16[10,1,8,128]{3,1,2,0:T(2,128)(2,1)S(1)}, u32[]{:S(2)}, u32[]{:S(2)}) collective-permute-start(bf16[10,1,8,128]{3,1,2,0:T(2,128)(2,1)S(1)} %get-tuple-element.81), channel_id=1, source_target_pairs={{4,0},{8,4},{12,8},{5,1},{9,5},{13,9},{6,2},{10,6},{14,10},{7,3},{... | collective-permute-start | bytes 61448 | tf_op jit(solution)/shard_map/ppermute | solution.py:17
  70.2 9.2 %collective-permute-start.4 = (bf16[10,18,1,128]{3,1,2,0:T(8,128)(2,1)S(1)}, bf16[10,18,1,128]{3,1,2,0:T(8,128)(2,1)S(1)}, u32[]{:S(2)}, u32[]{:S(2)}) collective-permute-start(bf16[10,18,1,128]{3,1,2,0:T(8,128)(2,1)S(1)} %get-tuple-element.73), channel_id=1, source_target_pairs={{0,1},{1,2},{2,3},{4,5},{5,6},{6,7},{8,9},{9,10},{10,11},{12,13},{... | collective-permute-start | bytes 138248 | tf_op jit(solution)/shard_map/ppermute | solution.py:14
  76.9 5.5 %collective-permute-start.5 = (bf16[10,18,1,128]{3,1,2,0:T(8,128)(2,1)S(1)}, bf16[10,18,1,128]{3,1,2,0:T(8,128)(2,1)S(1)}, u32[]{:S(2)}, u32[]{:S(2)}) collective-permute-start(bf16[10,18,1,128]{3,1,2,0:T(8,128)(2,1)S(1)} %get-tuple-element.72), channel_id=1, source_target_pairs={{1,0},{2,1},{3,2},{5,4},{6,5},{7,6},{9,8},{10,9},{11,10},{13,12},{... | collective-permute-start | bytes 138248 | tf_op jit(solution)/shard_map/ppermute | solution.py:17
  79.4 8.9 %copy-start.1 = (bf16[10,17,8,128]{3,1,2,0:T(8,128)(2,1)}, bf16[10,17,8,128]{3,1,2,0:T(8,128)(2,1)S(1)}, u32[]{:S(2)}) copy-start(bf16[10,17,8,128]{3,1,2,0:T(8,128)(2,1)S(1)} %get-tuple-element.79) | copy-start | bytes 1044484
  91.9 240.4 %all-reduce.6.cloned.1.call-start = ((), (), s32[]{:S(2)}) async-start(), calls=%async_computation.3 | async-start | bytes 524288
  107.5 351.9 %all-reduce.4.cloned.1.call-start = ((), (), s32[]{:S(2)}) async-start(), calls=%async_computation.2 | async-start | bytes 221184 | tf_op jit(solution)/shard_map/psum | solution.py:118
  107.8 1.1 copy-start.2
  (5 other events, 4.1 us)
Sparse Core Ops, SparseCore 0:
  92.0 83.0 reduce-scatter.1
  177.7 154.5 all-reduce.5
  335.2 124.2 all-reduce.3
where the time goes:
time: 469 us; the launch traced here: 467 us
  waiting for transfers between devices  298 us (64%)
  blocking collectives  59.6 us (13%)
  starting transfers between devices  39.7 us (8%)
  matrix products  28.8 us (6%)
  local copies, waits for them, and re-layouts  17.8 us (4%)
  between operations  15.9 us (3%)
  other arithmetic  8.08 us (2%)
    unnamed x4, waiting for transfers between devices  157 us
    psum x1, waiting for transfers between devices, body(): whole_conv, whole_down = lax.psum((conv_terms, down_terms), ('gy', 'gz'))  66.1 us
    psum x1, blocking collectives, body(): whole_conv, whole_down = lax.psum((conv_terms, down_terms), ('gy', 'gz'))  59.6 us
    reduce_scatter x1, waiting for transfers between devices, body(): lax.psum_scatter(whole_conv, 'gx', scatter_dimension=1, tiled=True)  55.9 us
    ppermute x6, starting transfers between devices, padded(): lax.ppermute(lax.slice_in_dim(block, block.shape[dim] - width, None, axis...  27 us
    ppermute x6, waiting for transfers between devices, padded(): lax.ppermute(lax.slice_in_dim(block, 0, width, axis=dim), axis, backward)  18.1 us
    ppermute x6, starting transfers between devices, padded(): lax.ppermute(lax.slice_in_dim(block, 0, width, axis=dim), axis, backward)  12.4 us
  transfers between devices with their start and end apart: 15, of which 9 were waited for; matrix products, arithmetic and copies ran while one was open for 6% of the time, Pallas kernels for 0%

commit v1 on v0

v1 whole, which is shorter than its diff:
```python
import jax
import jax.numpy as jnp
from jax import lax
from jax.experimental import pallas as pl
from jax.experimental.pallas import tpu as pltpu
from jax.sharding import PartitionSpec as P

BF = jnp.bfloat16
F32 = jnp.float32
MESH = pl.DeviceIdType.MESH

NGX, NGY, NGZ = 16, 4, 4
NEIGHBOURS = [
    (sx, sy, sz)
    for sz in (-1, 1, 0)
    for sy in (-1, 0, 1)
    for sx in (-1, 0, 1)
    if (sx, sy, sz) != (0, 0, 0)
]
GROUPS = [3, 4, 5, 0, 1, 2, 6, 7, 8]
SLOTS = [3 * g + 2 - b for g in GROUPS for b in range(3)] + [27, 28, 29, 30]


def dot(a, b, ca, cb):
    return lax.dot_general(a, b, (((ca,), (cb,)), ((), ())), preferred_element_type=F32)


def kernel(
    fine, occupied, w_down, w_conv, cot,
    out, d_fine, d_wconv, d_wdown,
    fine_v, wd_v, wc_v, cot_v,
    mp, ap, mz, az, mzr, azr, me_v, mo_v, ae_v, ao_v,
    zv, act_t, patch_t, acc, dz_v, grads,
    r0, p1, r1, s1acc, p2, r3, p3, r4,
    load_sem, mh_s, mh_r, ah_s, ah_r,
    s0_s, s0_r, s1_s, s1_r, s3_s, s3_r, s4_s, s4_r,
):
    gx, gy, gz = lax.axis_index("gx"), lax.axis_index("gy"), lax.axis_index("gz")
    yy, zhi, xx = gx // 4, lax.rem(gx, 4), gy
    zlo, core = gz // 2, lax.rem(gz, 2)
    zz = zhi * 2 + zlo

    def near(s):
        return (
            lax.rem(gx + s[0] + NGX, NGX),
            lax.rem(gy + s[1] + NGY, NGY),
            lax.rem(gz + s[2] + NGZ, NGZ),
        )

    other = (gx, gy, gz + 1 - 2 * core)

    def plane(n):
        tx, ty = lax.rem(xx + lax.rem(n, 4), 4), lax.rem(yy + n // 4, 4)
        return tx, ty, (ty * 4 + zhi, tx, gz)

    def column(n):
        tz = lax.rem(zz + n, 8)
        return tz // 2, (yy * 4 + tz // 2, gy, lax.rem(tz, 2) * 2 + core)

    def row(n):
        tx, tc = lax.rem(xx + n // 2, 4), lax.rem(core + lax.rem(n, 2), 2)
        return (gx, tx, zlo * 2 + tc)

    loads = [
        pltpu.make_async_copy(a, b, load_sem.at[i])
        for i, (a, b) in enumerate(((cot, cot_v), (fine, fine_v), (w_down, wd_v), (w_conv, wc_v)))
    ]
    for c in loads:
        c.start()

    barrier = pltpu.get_barrier_semaphore()

    def greet(device):
        pl.semaphore_signal(barrier, inc=1, device_id=device, device_id_type=MESH)

    for s in NEIGHBOURS:
        greet(near(s))
    greet(other)

    @pl.loop(1, 16)
    def _(n):
        greet(plane(n)[2])

    @pl.loop(1, 8)
    def _(n):
        greet(column(n)[1])

    @pl.loop(1, 8)
    def _(n):
        greet(row(n))

    o0 = occupied[0, 0, 0].astype(F32)
    o1 = occupied[0, 1, 0].astype(F32)
    rows = lax.broadcasted_iota(jnp.int32, (16, 8, 128), 0)
    occ = jnp.where(rows < 8, o0, o1)
    loads[0].wait()

    @pl.loop(0, 8)
    def _(x):
        m = cot_v[x].astype(F32) * occ
        mp[x + 1, 1:17] = m.astype(BF)
        mz[0, x] = m[:, 0:1, :]
        mz[1, x] = m[:, 7:8, :]

    pl.semaphore_wait(barrier, 26 + 1 + 15 + 7 + 7)

    def halo(pad, zs, zr, ss, rs):
        copies = []
        for i, (sx, sy, sz) in enumerate(NEIGHBOURS):
            sxs = {-1: slice(1, 2), 0: slice(1, 9), 1: slice(8, 9)}[sx]
            dxs = {-1: slice(9, 10), 0: slice(1, 9), 1: slice(0, 1)}[sx]
            sys_ = {-1: slice(1, 2), 0: slice(1, 17), 1: slice(16, 17)}[sy]
            dys = {-1: slice(17, 18), 0: slice(1, 17), 1: slice(0, 1)}[sy]
            if sz == 0:
                src = pad.at[sxs, sys_]
                dst = pad.at[dxs, dys]
            else:
                src = zs.at[(sz + 1) // 2, slice(sxs.start - 1, sxs.stop - 1),
                            slice(sys_.start - 1, sys_.stop - 1)]
                dst = zr.at[(1 - sz) // 2, dxs, dys]
            copies.append(
                pltpu.make_async_remote_copy(
                    src_ref=src, dst_ref=dst, send_sem=ss.at[i], recv_sem=rs.at[i],
                    device_id=near((sx, sy, sz)), device_id_type=MESH,
                )
            )
        for c in copies:
            c.start()
        return copies

    m_copies = halo(mp, mz, mzr, mh_s, mh_r)

    loads[1].wait()
    loads[2].wait()
    patches = [
        fine_v[:, a, :, b].reshape(1024, 128) for a in range(2) for b in range(2)
    ]
    z = dot(jnp.concatenate(patches, axis=1), wd_v[...].reshape(512, 128), 1, 0)
    zval = (z.reshape(8, 16, 8, 128) * occ[None]).astype(BF)
    act = jnp.maximum(zval.astype(F32), 0.0)
    zv[...] = zval
    ap[1:9, 1:17] = act.astype(BF)
    az[0] = act[:, :, 0:1, :]
    az[1] = act[:, :, 7:8, :]
    a_copies = halo(ap, az, azr, ah_s, ah_r)
    act_t[...] = act.reshape(1024, 128).T.astype(BF)
    for i in range(4):
        patch_t[i * 128 : (i + 1) * 128] = patches[i].T

    kk = lax.broadcasted_iota(jnp.int32, (18, 8, 128), 1)
    yi = lax.broadcasted_iota(jnp.int32, (18, 8, 128), 0)
    inside_y = jnp.logical_and(
        jnp.logical_or(yi > 0, gy > 0), jnp.logical_or(yi < 17, gy < NGY - 1)
    )

    def build(pad, zr, even, odd):
        @pl.loop(0, 10)
        def _(x):
            inside_x = jnp.logical_and(
                jnp.logical_or(x > 0, gx > 0), jnp.logical_or(x < 9, gx < NGX - 1)
            )
            keep = jnp.where(jnp.logical_and(inside_y, inside_x), 1.0, 0.0)
            low = jnp.where(gz > 0, 1.0, 0.0)
            high = jnp.where(gz < NGZ - 1, 1.0, 0.0)
            m = pad[x].astype(F32)
            lo = jnp.where(kk == 0, zr[0, x] * low, pltpu.roll(m, 1, 1)) * keep
            hi = jnp.where(kk == 7, zr[1, x] * high, pltpu.roll(m, 7, 1)) * keep
            for b, v in enumerate((lo, m * keep, hi)):
                even[x, :, b * 128 : (b + 1) * 128] = v.reshape(144, 128).astype(BF)
                odd[x, :, b * 128 : (b + 1) * 128] = v[1:17].reshape(128, 128).astype(BF)

    def cut(even, odd, ox, oy):
        if oy == 1:
            return odd[ox : ox + 8].reshape(1024, 384)
        return even[ox : ox + 8, oy * 8 : oy * 8 + 128].reshape(1024, 384)

    def behind(g):
        return cut(me_v, mo_v, 2 - g // 3, 2 - g % 3)

    for c in m_copies:
        c.wait_recv()
    build(mp, mzr, me_v, mo_v)

    def conv_grads(lo, hi):
        for i in range(lo, hi):
            d = dot(act_t[...], behind(GROUPS[i]), 1, 0)
            for b in range(3):
                grads[3 * i + b] = d[:, b * 128 : (b + 1) * 128].astype(BF)

    def s0(j):
        return pltpu.make_async_remote_copy(
            src_ref=grads.at[pl.ds(8 * j + 4 - 4 * core, 4)], dst_ref=r0.at[j],
            send_sem=s0_s.at[j], recv_sem=s0_r.at[j], device_id=other, device_id_type=MESH,
        )

    def s1(j, n):
        tx, ty, device = plane(n)
        return pltpu.make_async_remote_copy(
            src_ref=p1.at[j, tx, pl.ds(pl.multiple_of(ty * 32, 32), 32)], dst_ref=r1.at[j, n],
            send_sem=s1_s.at[j, n], recv_sem=s1_r.at[j, n],
            device_id=device, device_id_type=MESH,
        )

    def s0_finish(j):
        s0(j).wait_recv()
        p1[j] = (grads[pl.ds(8 * j + 4 * core, 4)].astype(F32) + r0[j].astype(F32)).astype(BF)

        @pl.loop(1, 16)
        def _(n):
            s1(j, n).start()

    def s1_finish(j):
        @pl.loop(1, 16)
        def _(n):
            s1(j, n).wait_recv()

        total = p1[j, xx, pl.ds(pl.multiple_of(yy * 32, 32), 32)].astype(F32)
        for n in range(1, 16):
            total = total + r1[j, n].astype(F32)
        s1acc[j] = total

    conv_grads(0, 3)
    s0(0).start()
    conv_grads(3, 6)
    s0(1).start()
    s0_finish(0)

    for g in range(0, 9, 2):
        pair = [g, g + 1] if g < 8 else [8]
        left = jnp.concatenate([behind(h) for h in pair], axis=1)
        right = jnp.concatenate([wc_v[3 * h + 2 - b] for h in pair for b in range(3)], axis=1)
        if g == 0:
            loads[3].wait()
            right = jnp.concatenate([wc_v[3 * h + 2 - b] for h in pair for b in range(3)], axis=1)
            acc[...] = dot(left, right, 1, 1)
        else:
            acc[...] += dot(left, right, 1, 1)
    s0_finish(1)
    d_act = acc[...].reshape(8, 16, 8, 128)
    positive = zv[...].astype(F32) > 0
    dz = occ[None] * (cot_v[...].astype(F32) + jnp.where(positive, d_act, 0.0))
    dz_v[...] = dz.reshape(1024, 128).astype(BF)
    d = dot(patch_t[...], dz_v[...], 1, 0)
    for i in range(4):
        grads[27 + i] = d[i * 128 : (i + 1) * 128].astype(BF)
    grads[31] = jnp.zeros((128, 128), BF)
    conv_grads(6, 8)
    s0(2).start()
    conv_grads(8, 9)
    s0(3).start()
    s0_finish(2)

    s0_finish(3)
    d = dot(dz_v[...], wd_v[...].reshape(512, 128), 1, 1)
    for a in range(2):
        for b in range(2):
            i = 2 * a + b
            d_fine[:, a, :, b] = d[:, i * 128 : (i + 1) * 128].reshape(8, 16, 8, 128).astype(BF)

    for c in a_copies:
        c.wait_recv()
    build(ap, azr, ae_v, ao_v)
    for g in range(0, 9, 2):
        pair = [g, g + 1] if g < 8 else [8]
        left = jnp.concatenate([cut(ae_v, ao_v, h // 3, h % 3) for h in pair], axis=1)
        right = wc_v[3 * g : 3 * g + 3 * len(pair)].reshape(384 * len(pair), 128)
        if g == 0:
            acc[...] = dot(left, right, 1, 0)
        else:
            acc[...] += dot(left, right, 1, 0)
    out[...] = (
        zv[...].astype(F32) + occ[None] * acc[...].reshape(8, 16, 8, 128)
    ).astype(BF)

    for j in range(4):
        s1_finish(j)
    for h in range(4):
        p2[h] = jnp.concatenate([s1acc[j, h * 8 : h * 8 + 8] for j in range(4)], axis=0).astype(BF)

    def s3(n):
        h, device = column(n)
        return pltpu.make_async_remote_copy(
            src_ref=p2.at[h], dst_ref=r3.at[n], send_sem=s3_s.at[n], recv_sem=s3_r.at[n],
            device_id=device, device_id_type=MESH,
        )

    @pl.loop(1, 8)
    def _(n):
        s3(n).start()

    @pl.loop(1, 8)
    def _(n):
        s3(n).wait_recv()

    total = p2[zhi].astype(F32)
    for n in range(1, 8):
        total = total + r3[n].astype(F32)
    mine = total.astype(BF)
    p3[...] = mine
    r4[xx * 2 + core] = mine

    def s4(n):
        return pltpu.make_async_remote_copy(
            src_ref=p3, dst_ref=r4.at[xx * 2 + core], send_sem=s4_s.at[n], recv_sem=s4_r.at[n],
            device_id=row(n), device_id_type=MESH,
        )

    @pl.loop(1, 8)
    def _(n):
        s4(n).start()

    @pl.loop(1, 8)
    def _(n):
        s4(n).wait_recv()

    scale = float(262144) ** -0.5
    for x in range(4):
        for c in range(2):
            v = r4[x * 2 + c].astype(F32) * scale
            for j in range(4):
                slot = 8 * j + 4 * c + x
                if slot == 31:
                    continue
                tap = SLOTS[slot]
                if tap < 27:
                    d_wconv[tap] = v[8 * j : 8 * j + 8]
                else:
                    d_wdown[tap - 27] = v[8 * j : 8 * j + 8]

    for c in m_copies + a_copies:
        c.wait_send()
    for j in range(4):
        s0(j).wait_send()

        @pl.loop(1, 16)
        def _(n):
            s1(j, n).wait_send()

    @pl.loop(1, 8)
    def _(n):
        s3(n).wait_send()
        s4(n).wait_send()


def body(fine, occupied, w_down, w_conv, cotangent):
    fine = fine.reshape(8, 2, 16, 2, 8, 128)
    vm = pltpu.VMEM
    dma = pltpu.SemaphoreType.DMA
    scratch = [
        vm(fine.shape, BF), vm(w_down.shape, BF), vm(w_conv.shape, BF), vm(cotangent.shape, BF),
        vm((10, 18, 8, 128), BF), vm((10, 18, 8, 128), BF),
        vm((2, 8, 16, 1, 128), F32), vm((2, 8, 16, 1, 128), F32),
        vm((2, 10, 18, 1, 128), F32), vm((2, 10, 18, 1, 128), F32),
        vm((10, 144, 384), BF), vm((10, 128, 384), BF),
        vm((10, 144, 384), BF), vm((10, 128, 384), BF),
        vm((8, 16, 8, 128), BF),
        vm((128, 1024), BF), vm((512, 1024), BF),
        vm((1024, 128), F32), vm((1024, 128), BF),
        vm((32, 128, 128), BF),
        vm((4, 4, 128, 128), BF), vm((4, 4, 128, 128), BF),
        vm((4, 16, 32, 128), BF), vm((4, 32, 128), F32),
        vm((4, 32, 128), BF), vm((8, 32, 128), BF),
        vm((32, 128), BF), vm((8, 32, 128), BF),
        dma((4,)), dma((26,)), dma((26,)), dma((26,)), dma((26,)),
        dma((4,)), dma((4,)), dma((4, 16)), dma((4, 16)),
        dma((8,)), dma((8,)), dma((8,)), dma((8,)),
    ]
    anym = pl.BlockSpec(memory_space=pl.ANY)
    vmem = pl.BlockSpec(memory_space=pltpu.VMEM)
    smem = pl.BlockSpec(memory_space=pltpu.SMEM)
    out, d_fine, d_wconv, d_wdown = pl.pallas_call(
        kernel,
        out_shape=(
            jax.ShapeDtypeStruct(cotangent.shape, BF),
            jax.ShapeDtypeStruct(fine.shape, BF),
            jax.ShapeDtypeStruct((27, 8, 128), F32),
            jax.ShapeDtypeStruct((4, 8, 128), F32),
        ),
        in_specs=[anym, smem, anym, anym, anym],
        out_specs=(vmem, vmem, vmem, vmem),
        scratch_shapes=scratch,
        compiler_params=pltpu.CompilerParams(
            collective_id=0, has_side_effects=True, vmem_limit_bytes=48 * 1024 * 1024
        ),
    )(fine, occupied, w_down, w_conv, cotangent)
    return out, d_fine.reshape(16, 32, 8, 128), d_wconv, d_wdown


def solution(mesh):
    in_specs = (P("gx", "gy", "gz", None), P("gx", "gy", "gz"), P(), P(), P("gx", "gy", "gz", None))
    out_specs = (
        P("gx", "gy", "gz", None),
        P("gx", "gy", "gz", None),
        P(None, "gx", None),
        P(None, "gx", None),
    )
    return jax.shard_map(body, mesh=mesh, in_specs=in_specs, out_specs=out_specs, check_vma=False)
```

time: 469 us -> 57.7 us (0.12)
  waiting for transfers between devices: 298 us -> 0 us
  blocking collectives: 59.6 us -> 0 us
  Pallas kernels: 0 us -> 48.9 us
  starting transfers between devices: 39.7 us -> 0 us
  matrix products: 28.8 us -> 0 us
  between operations: 15.9 us -> 0.65 us
  local copies, waits for them, and re-layouts: 17.8 us -> 7.91 us
  other arithmetic: 8.08 us -> 0 us
    unnamed x4 -> x0, waiting for transfers between devices: 157 us -> none
    psum x1 -> x0, waiting for transfers between devices: 66.1 us -> none  [body(): whole_conv, whole_down = lax.psum((conv_terms, down_terms), ('gy', 'gz'))]
    psum x1 -> x0, blocking collectives: 59.6 us -> none  [body(): whole_conv, whole_down = lax.psum((conv_terms, down_terms), ('gy', 'gz'))]
    reduce_scatter x1 -> x0, waiting for transfers between devices: 55.9 us -> none  [body(): lax.psum_scatter(whole_conv, 'gx', scatter_dimension=1, tiled=True)]
    pallas_call x0 -> x1, Pallas kernels: none -> 48.9 us  [body(): pl.pallas_call(kernel, out_shape=(jax.ShapeDtypeStruct(cotangent.shape, B...]
    ppermute x12 -> x0, starting transfers between devices: 39.4 us -> none  [the longest x6 27 us: padded(): lax.ppermute(lax.slice_in_dim(block, block.shape[dim] - width, None, axis...]
    dot_general x93 -> x0, matrix products: 28.8 us -> none  [the longest x27 7.28 us: section_block(): lax.dot_general(ahead, masked_flat, (((0,), (0,)), ((), ())), preferred_e...]
    ppermute x12 -> x0, waiting for transfers between devices: 18.2 us -> none  [the longest x6 18.1 us: padded(): lax.ppermute(lax.slice_in_dim(block, 0, width, axis=dim), axis, backward)]
  transfers between devices with their start and end apart: 15 -> 0, of which waited for: 9 -> 0; matrix products, arithmetic and copies ran while one was open for 6% -> 0% of each run, Pallas kernels for 0% -> 0%
where the time goes in v1:
time: 57.7 us; the launch traced here: 57.5 us
  Pallas kernels  48.9 us (85%)
  local copies, waits for them, and re-layouts  7.91 us (14%)
  between operations  0.65 us (1%)
    pallas_call x1, Pallas kernels, body(): pl.pallas_call(kernel, out_shape=(jax.ShapeDtypeStruct(cotangent.shape, B...  48.9 us
    unnamed x15, local copies, waits for them, and re-layouts  7.91 us

profile of v1, /device:TPU:1, one launch (start us, length us, event | category | flops | bytes accessed | tf_op | source)
XLA Modules:
  0.0 57.5 jit_solution(17493455194025358355)
XLA Ops:
  0.6 0.0 copy-start.4
  0.6 0.6 %copy-done.4 = s32[1,2,1]{1,2,0:T(1,128)S(1)} copy-done((s32[1,2,1]{1,2,0:T(1,128)S(1)}, s32[1,2,1]{1,2,0:T(1,128)}, u32[]{:S(2)}) %copy-start.4) | copy-done | bytes 32
  1.3 0.1 copy.9.occupied
  1.4 0.0 copy-start
  1.4 1.2 %copy-done = bf16[16,32,8,128]{3,2,1,0:T(8,128)(2,1)S(1)} copy-done((bf16[16,32,8,128]{3,2,1,0:T(8,128)(2,1)S(1)}, bf16[16,32,8,128]{3,2,1,0:T(8,128)(2,1)}, u32[]{:S(2)}) %copy-start) | copy-done | bytes 1048600
  2.6 0.0 copy-start.1
  2.6 1.2 %copy-done.1 = bf16[27,128,128]{2,1,0:T(8,128)(2,1)S(1)} copy-done((bf16[27,128,128]{2,1,0:T(8,128)(2,1)S(1)}, bf16[27,128,128]{2,1,0:T(8,128)(2,1)}, u32[]{:S(2)}) %copy-start.1) | copy-done | bytes 884760
  3.8 0.0 copy-start.2
  3.8 0.9 %copy-done.2 = bf16[8,16,8,128]{3,2,1,0:T(8,128)(2,1)S(1)} copy-done((bf16[8,16,8,128]{3,2,1,0:T(8,128)(2,1)S(1)}, bf16[8,16,8,128]{3,2,1,0:T(8,128)(2,1)}, u32[]{:S(2)}) %copy-start.2) | copy-done | bytes 262168
  4.7 0.0 copy-start.3
  4.7 0.9 %copy-done.3 = bf16[4,128,128]{2,1,0:T(8,128)(2,1)S(1)} copy-done((bf16[4,128,128]{2,1,0:T(8,128)(2,1)S(1)}, bf16[4,128,128]{2,1,0:T(8,128)(2,1)}, u32[]{:S(2)}) %copy-start.3) | copy-done | bytes 131096
  5.6 48.9 %shard_map.84 = (bf16[8,16,8,128]{3,2,1,0:T(8,128)(2,1)S(1)}, bf16[8,2,16,2,8,128]{5,4,3,2,1,0:T(8,128)(2,1)S(1)}, f32[27,8,128]{2,1,0:T(8,128)S(1)}, f32[4,8,128]{2,1,0:T(8,128)S(1)}) custom-call(bf16[8,2,16,2,8,128]{5,4,3,2,1,0:T(8,128)(2,1)S(1)} %bitcast.2, s32[1,2,1]{2,1,0:T(2,128)S(1)} %copy.9.occupied, bf16[4,128,128]{2,1,0:T(8,128)(2,1)S(1)} %copy-done.3, ...), custom_call_target="tpu_custom_call" | custom-call | tf_op jit(solution)/shard_map/pallas_call | solution.py:371
  54.6 0.7 %copy.14 = bf16[8,16,8,128]{3,2,1,0:T(8,128)(2,1)} copy(bf16[8,16,8,128]{3,2,1,0:T(8,128)(2,1)S(1)} %get-tuple-element.16) | data formatting | bytes 524288
  55.3 1.0 %copy.15 = bf16[16,32,8,128]{3,2,1,0:T(8,128)(2,1)} copy(bf16[16,32,8,128]{3,2,1,0:T(8,128)(2,1)S(1)} %bitcast.3) | data formatting | bytes 2097152
  56.2 0.6 %copy.16 = f32[27,8,128]{2,1,0:T(8,128)} copy(f32[27,8,128]{2,1,0:T(8,128)S(1)} %get-tuple-element.18) | data formatting | bytes 221184
  56.9 0.6 %copy.17 = f32[4,8,128]{2,1,0:T(8,128)} copy(f32[4,8,128]{2,1,0:T(8,128)S(1)} %get-tuple-element.19) | data formatting | bytes 32768
Async XLA Ops:
  0.6 0.7 %copy-start.4 = (s32[1,2,1]{1,2,0:T(1,128)S(1)}, s32[1,2,1]{1,2,0:T(1,128)}, u32[]{:S(2)}) copy-start(s32[1,2,1]{1,2,0:T(1,128)} %param.6) | copy-start | bytes 28
  1.4 1.2 %copy-start = (bf16[16,32,8,128]{3,2,1,0:T(8,128)(2,1)S(1)}, bf16[16,32,8,128]{3,2,1,0:T(8,128)(2,1)}, u32[]{:S(2)}) copy-start(bf16[16,32,8,128]{3,2,1,0:T(8,128)(2,1)} %param.5) | copy-start | bytes 3145732
  2.6 1.2 %copy-start.1 = (bf16[27,128,128]{2,1,0:T(8,128)(2,1)S(1)}, bf16[27,128,128]{2,1,0:T(8,128)(2,1)}, u32[]{:S(2)}) copy-start(bf16[27,128,128]{2,1,0:T(8,128)(2,1)} %w_conv.1) | copy-start | bytes 2654212
  3.8 0.9 %copy-start.2 = (bf16[8,16,8,128]{3,2,1,0:T(8,128)(2,1)S(1)}, bf16[8,16,8,128]{3,2,1,0:T(8,128)(2,1)}, u32[]{:S(2)}) copy-start(bf16[8,16,8,128]{3,2,1,0:T(8,128)(2,1)} %cot.1) | copy-start | bytes 786436
  4.7 0.9 %copy-start.3 = (bf16[4,128,128]{2,1,0:T(8,128)(2,1)S(1)}, bf16[4,128,128]{2,1,0:T(8,128)(2,1)}, u32[]{:S(2)}) copy-start(bf16[4,128,128]{2,1,0:T(8,128)(2,1)} %w_down.1) | copy-start | bytes 393220

commit v2 on v1

v2 whole, which is shorter than its diff:
```python
import jax
import jax.numpy as jnp
from jax import lax
from jax.experimental import pallas as pl
from jax.experimental.pallas import tpu as pltpu
from jax.sharding import PartitionSpec as P

BF = jnp.bfloat16
F32 = jnp.float32
MESH = pl.DeviceIdType.MESH

NGX, NGY, NGZ = 16, 4, 4
NEIGHBOURS = [
    (sx, sy, sz)
    for sx in (-1, 1, 0)
    for sz in (-1, 1, 0)
    for sy in (-1, 1, 0)
    if (sx, sy, sz) != (0, 0, 0)
]
FAR = 18
GROUPS = [3, 4, 5, 0, 1, 2, 6, 7, 8]
SLOTS = [3 * g + 2 - b for g in GROUPS for b in range(3)] + [27, 28, 29, 30]


def dot(a, b, ca, cb):
    return lax.dot_general(a, b, (((ca,), (cb,)), ((), ())), preferred_element_type=F32)


def kernel(
    fine, occupied, w_down, w_conv, cot,
    out_h, d_fine_h, d_wconv_h, d_wdown_h,
    out, d_fine, d_wconv, d_wdown, store_sem, fine_v, wd_v, wc_v, cot_v,
    mp, ap, mz, az, mzr, azr, me_v, mo_v, ae_v, ao_v,
    zv, act_t, patch_t, acc, dz_v, grads,
    r0, p1, r1, p2, r3, p3, r4, gsum, dsum,
    occ_v, load_sem, halo_s, mh_r, ah_r, s0_s, s0_r, s1_s, s1_r, s3_s, s3_r, s4_s, s4_r,
):
    gx, gy, gz = lax.axis_index("gx"), lax.axis_index("gy"), lax.axis_index("gz")
    yy, zhi, xx = gx // 4, lax.rem(gx, 4), gy
    zlo, core = gz // 2, lax.rem(gz, 2)
    zz = zhi * 2 + zlo

    def near(s):
        return (
            lax.rem(gx + s[0] + NGX, NGX),
            lax.rem(gy + s[1] + NGY, NGY),
            lax.rem(gz + s[2] + NGZ, NGZ),
        )

    other = (gx, gy, gz + 1 - 2 * core)

    def plane(n):
        tx, ty = lax.rem(xx + lax.rem(n, 4), 4), lax.rem(yy + n // 4, 4)
        return tx, ty, (ty * 4 + zhi, tx, gz)

    def column(n):
        tz = lax.rem(zz + n, 8)
        return tz // 2, (yy * 4 + tz // 2, gy, lax.rem(tz, 2) * 2 + core)

    def row(n):
        tx, tc = lax.rem(xx + n // 2, 4), lax.rem(core + lax.rem(n, 2), 2)
        return (gx, tx, zlo * 2 + tc)

    loads = [
        pltpu.make_async_copy(a, b, load_sem.at[i])
        for i, (a, b) in enumerate(((cot, cot_v), (fine, fine_v), (w_down, wd_v), (w_conv, wc_v), (occupied, occ_v)))
    ]
    for c in loads:
        c.start()

    barrier = pltpu.get_barrier_semaphore()

    def greet(device):
        pl.semaphore_signal(barrier, inc=1, device_id=device, device_id_type=MESH)

    for s in NEIGHBOURS:
        greet(near(s))
    greet(other)

    @pl.loop(1, 16)
    def _(n):
        greet(plane(n)[2])

    @pl.loop(1, 8)
    def _(n):
        greet(column(n)[1])

    @pl.loop(1, 8)
    def _(n):
        greet(row(n))

    loads[4].wait()
    o0 = occ_v[0, 0, 0].astype(F32)
    o1 = occ_v[0, 0, 1].astype(F32)
    rows = lax.broadcasted_iota(jnp.int32, (16, 8, 128), 0)
    occ = jnp.where(rows < 8, o0, o1)
    loads[0].wait()

    @pl.loop(0, 8)
    def _(x):
        m = cot_v[x].astype(F32) * occ
        mp[x + 1, 1:17] = m.astype(BF)
        mz[0, x] = m[:, 0:1, :]
        mz[1, x] = m[:, 7:8, :]

    pl.semaphore_wait(barrier, 26 + 1 + 15 + 7 + 7)

    def halo(pad, zs, zr, rs):
        copies = []
        for i, (sx, sy, sz) in enumerate(NEIGHBOURS):
            sxs = {-1: slice(1, 2), 0: slice(1, 9), 1: slice(8, 9)}[sx]
            dxs = {-1: slice(9, 10), 0: slice(1, 9), 1: slice(0, 1)}[sx]
            sys_ = {-1: slice(1, 2), 0: slice(1, 17), 1: slice(16, 17)}[sy]
            dys = {-1: slice(17, 18), 0: slice(1, 17), 1: slice(0, 1)}[sy]
            if sz == 0:
                src = pad.at[sxs, sys_]
                dst = pad.at[dxs, dys]
            else:
                src = zs.at[(sz + 1) // 2, slice(sxs.start - 1, sxs.stop - 1),
                            slice(sys_.start - 1, sys_.stop - 1)]
                dst = zr.at[(1 - sz) // 2, dxs, dys]
            copies.append(
                pltpu.make_async_remote_copy(
                    src_ref=src, dst_ref=dst, send_sem=halo_s, recv_sem=rs.at[0 if i < FAR else 1],
                    device_id=near((sx, sy, sz)), device_id_type=MESH,
                )
            )
        for c in copies:
            c.start()

    def landed(sem, ref):
        pltpu.make_async_copy(ref, ref, sem).wait()

    far_bytes, near_bytes = acc.at[0:216], acc.at[0:352]

    halo(mp, mz, mzr, mh_r)

    loads[1].wait()
    loads[2].wait()
    patches = [
        fine_v[:, a, :, b].reshape(1024, 128) for a in range(2) for b in range(2)
    ]
    z = dot(jnp.concatenate(patches, axis=1), wd_v[...].reshape(512, 128), 1, 0)
    zval = (z.reshape(8, 16, 8, 128) * occ[None]).astype(BF)
    act = jnp.maximum(zval.astype(F32), 0.0)
    zv[...] = zval
    ap[1:9, 1:17] = act.astype(BF)
    az[0] = act[:, :, 0:1, :]
    az[1] = act[:, :, 7:8, :]
    halo(ap, az, azr, ah_r)
    act_t[...] = act.reshape(1024, 128).T.astype(BF)
    for i in range(4):
        patch_t[i * 128 : (i + 1) * 128] = patches[i].T

    kk = lax.broadcasted_iota(jnp.int32, (18, 8, 128), 1)
    yi = lax.broadcasted_iota(jnp.int32, (18, 8, 128), 0)
    inside_y = jnp.logical_and(
        jnp.logical_or(yi > 0, gy > 0), jnp.logical_or(yi < 17, gy < NGY - 1)
    )

    def build(pad, zr, even, odd, first, last):
        @pl.loop(first, last)
        def _(x):
            inside_x = jnp.logical_and(
                jnp.logical_or(x > 0, gx > 0), jnp.logical_or(x < 9, gx < NGX - 1)
            )
            keep = jnp.where(jnp.logical_and(inside_y, inside_x), 1.0, 0.0)
            low = jnp.where(gz > 0, 1.0, 0.0)
            high = jnp.where(gz < NGZ - 1, 1.0, 0.0)
            m = pad[x].astype(F32)
            lo = jnp.where(kk == 0, zr[0, x] * low, pltpu.roll(m, 1, 1)) * keep
            hi = jnp.where(kk == 7, zr[1, x] * high, pltpu.roll(m, 7, 1)) * keep
            for b, v in enumerate((lo, m * keep, hi)):
                even[x, :, b * 128 : (b + 1) * 128] = v.reshape(144, 128).astype(BF)
                odd[x, :, b * 128 : (b + 1) * 128] = v[1:17].reshape(128, 128).astype(BF)

    def cut(even, odd, first, count, oy):
        if oy == 1:
            return odd[first : first + count].reshape(count * 128, 384)
        return even[first : first + count, oy * 8 : oy * 8 + 128].reshape(count * 128, 384)

    own = {0: (2, 0, 7), 1: (1, 0, 8), 2: (1, 1, 7)}
    edge = {0: (9, 7, 1), 2: (0, 0, 1)}

    def conv_grad(g, where):
        first, mine, count = where[g // 3]
        return dot(
            act_t[:, mine * 128 : (mine + count) * 128],
            cut(me_v, mo_v, first, count, 2 - g % 3), 1, 0,
        )

    def back(dx, where):
        first, mine, count = where[dx]
        left = jnp.concatenate(
            [cut(me_v, mo_v, first, count, 2 - dy) for dy in range(3)], axis=1
        )
        right = jnp.concatenate(
            [wc_v[9 * dx + 3 * dy + 2 - b] for dy in range(3) for b in range(3)], axis=1
        )
        return slice(mine * 128, (mine + count) * 128), dot(left, right, 1, 1)

    def dz_of(first, last):
        d_act = acc[first * 128 : last * 128].reshape(last - first, 16, 8, 128)
        positive = zv[first:last].astype(F32) > 0
        dz = occ[None] * (cot_v[first:last].astype(F32) + jnp.where(positive, d_act, 0.0))
        dz_v[first * 128 : last * 128] = dz.reshape((last - first) * 128, 128).astype(BF)

    def s0(j):
        return pltpu.make_async_remote_copy(
            src_ref=grads.at[pl.ds(8 * j + 4 - 4 * core, 4)], dst_ref=r0.at[j],
            send_sem=s0_s, recv_sem=s0_r.at[j], device_id=other, device_id_type=MESH,
        )

    def s1(j, n):
        tx, ty, device = plane(n)
        return pltpu.make_async_remote_copy(
            src_ref=p1.at[j, tx, pl.ds(pl.multiple_of(ty * 32, 32), 32)], dst_ref=r1.at[j, n],
            send_sem=s1_s, recv_sem=s1_r.at[j],
            device_id=device, device_id_type=MESH,
        )

    def s0_finish(j):
        s0(j).wait_recv()
        p1[j] = (grads[pl.ds(8 * j + 4 * core, 4)].astype(F32) + r0[j].astype(F32)).astype(BF)

        @pl.loop(1, 16)
        def _(n):
            s1(j, n).start()

    def s1_finish(j):
        landed(s1_r.at[j], r1.at[j, pl.ds(1, 15)])

        total = p1[j, xx, pl.ds(pl.multiple_of(yy * 32, 32), 32)].astype(F32)
        for n in range(1, 16):
            total = total + r1[j, n].astype(F32)
        return total

    def s3(i, n):
        h, device = column(n)
        return pltpu.make_async_remote_copy(
            src_ref=p2.at[i, h], dst_ref=r3.at[i, n],
            send_sem=s3_s, recv_sem=s3_r.at[i],
            device_id=device, device_id_type=MESH,
        )

    def s4(i, n):
        return pltpu.make_async_remote_copy(
            src_ref=p3.at[i], dst_ref=r4.at[i, xx * 2 + core],
            send_sem=s4_s, recv_sem=s4_r.at[i],
            device_id=row(n), device_id_type=MESH,
        )

    def s3_start(i):
        low, high = s1_finish(2 * i), s1_finish(2 * i + 1)
        for h in range(4):
            p2[i, h] = jnp.concatenate(
                [low[h * 8 : h * 8 + 8], high[h * 8 : h * 8 + 8]], axis=0
            ).astype(BF)

        @pl.loop(1, 8)
        def _(n):
            s3(i, n).start()

    def s4_start(i):
        landed(s3_r.at[i], r3.at[i, pl.ds(1, 7)])

        total = p2[i, zhi].astype(F32)
        for n in range(1, 8):
            total = total + r3[i, n].astype(F32)
        mine = total.astype(BF)
        p3[i] = mine
        r4[i, xx * 2 + core] = mine

        @pl.loop(1, 8)
        def _(n):
            s4(i, n).start()

    def s4_finish(i):
        landed(s4_r.at[i], r4.at[i, pl.ds(1, 7)])

        for x in range(4):
            for c in range(2):
                v = r4[i, x * 2 + c].astype(F32) * (262144.0 ** -0.5)
                for h in range(2):
                    slot = 8 * (2 * i + h) + 4 * c + x
                    if slot == 31:
                        continue
                    tap = SLOTS[slot]
                    if tap < 27:
                        d_wconv[tap] = v[8 * h : 8 * h + 8]
                    else:
                        d_wdown[tap - 27] = v[8 * h : 8 * h + 8]

    def put(i, d):
        for b in range(3):
            grads[3 * i + b] = d[:, b * 128 : (b + 1) * 128].astype(BF)

    landed(mh_r.at[1], near_bytes)
    build(mp, mzr, me_v, mo_v, 1, 9)
    for i in range(3):
        put(i, conv_grad(GROUPS[i], own))
    s0(0).start()
    loads[3].wait()
    acc[...] = back(1, own)[1]
    s0_finish(0)
    for i in range(3, 9):
        gsum[i - 3] = conv_grad(GROUPS[i], own)
    for dx in (0, 2):
        where, d = back(dx, own)
        acc[where] += d
    dz_of(1, 7)
    dsum[...] = dot(patch_t[:, 128:896], dz_v[128:896], 1, 0)

    landed(mh_r.at[0], far_bytes)
    build(mp, mzr, me_v, mo_v, 0, 1)
    build(mp, mzr, me_v, mo_v, 9, 10)
    for i in range(3, 9):
        put(i, gsum[i - 3] + conv_grad(GROUPS[i], edge))
        if i == 5:
            s0(1).start()
        if i == 7:
            s0(2).start()
    for dx in (0, 2):
        where, d = back(dx, edge)
        acc[where] += d
    dz_of(0, 1)
    dz_of(7, 8)
    d = dsum[...] + dot(
        jnp.concatenate([patch_t[:, :128], patch_t[:, 896:]], axis=1),
        jnp.concatenate([dz_v[:128], dz_v[896:]], axis=0), 1, 0,
    )
    for i in range(4):
        grads[27 + i] = d[i * 128 : (i + 1) * 128].astype(BF)
    grads[31] = jnp.zeros((128, 128), BF)
    s0(3).start()
    s0_finish(1)
    s0_finish(2)
    s0_finish(3)

    d = dot(dz_v[...], wd_v[...].reshape(512, 128), 1, 1)
    for a in range(2):
        for b in range(2):
            i = 2 * a + b
            d_fine[:, a, :, b] = d[:, i * 128 : (i + 1) * 128].reshape(8, 16, 8, 128).astype(BF)

    def store(i):
        pairs = ((out, out_h), (d_fine, d_fine_h), (d_wconv, d_wconv_h), (d_wdown, d_wdown_h))
        return pltpu.make_async_copy(*pairs[i], store_sem.at[i])

    store(1).start()

    landed(ah_r.at[0], far_bytes)
    landed(ah_r.at[1], near_bytes)
    build(ap, azr, ae_v, ao_v, 0, 10)
    s3_start(0)
    for g in range(0, 9, 2):
        pair = [g, g + 1] if g < 8 else [8]
        left = jnp.concatenate([cut(ae_v, ao_v, h // 3, 8, h % 3) for h in pair], axis=1)
        right = wc_v[3 * g : 3 * g + 3 * len(pair)].reshape(384 * len(pair), 128)
        if g == 0:
            acc[...] = dot(left, right, 1, 0)
        else:
            acc[...] += dot(left, right, 1, 0)
    out[...] = (
        zv[...].astype(F32) + occ[None] * acc[...].reshape(8, 16, 8, 128)
    ).astype(BF)
    store(0).start()
    s3_start(1)
    s4_start(0)
    s4_start(1)
    s4_finish(0)
    s4_finish(1)
    store(2).start()
    store(3).start()

    landed(halo_s, acc.at[0:568])
    landed(halo_s, acc.at[0:568])
    landed(s0_s, r0)
    landed(s1_s, r1.at[:, pl.ds(1, 15)])
    landed(s3_s, r3.at[:, pl.ds(1, 7)])
    landed(s4_s, r4.at[:, pl.ds(1, 7)])
    for i in range(4):
        store(i).wait()


PARTS = (1, 4, 1, 1)


def publish_kernel(*refs):
    ins, outs, held = refs[:4], refs[4:8], refs[8:12]
    load_sem, store_sem = refs[12:]
    pieces = []
    for i, parts in enumerate(PARTS):
        size = ins[i].shape[0] // parts
        for p in range(parts):
            at = pl.ds(p * size, size)
            k = len(pieces)
            pieces.append((
                pltpu.make_async_copy(ins[i].at[at], held[i].at[at], load_sem.at[k]),
                pltpu.make_async_copy(held[i].at[at], outs[i].at[at], store_sem.at[k]),
            ))
    for load, _ in pieces:
        load.start()
    for load, store in pieces:
        load.wait()
        store.start()
    for _, store in pieces:
        store.wait()


def publish(*arrays):
    anym = pl.BlockSpec(memory_space=pl.ANY)
    return pl.pallas_call(
        publish_kernel,
        out_shape=tuple(jax.ShapeDtypeStruct(a.shape, a.dtype) for a in arrays),
        in_specs=[anym] * 4,
        out_specs=(anym,) * 4,
        scratch_shapes=[pltpu.VMEM(a.shape, a.dtype) for a in arrays]
        + [pltpu.SemaphoreType.DMA((sum(PARTS),))] * 2,
        compiler_params=pltpu.CompilerParams(vmem_limit_bytes=56 * 1024 * 1024),
    )(*arrays)


def body(fine, occupied, w_down, w_conv, cotangent):
    fine = fine.reshape(8, 2, 16, 2, 8, 128)
    vm = pltpu.VMEM
    dma = pltpu.SemaphoreType.DMA
    scratch = [
        vm(cotangent.shape, BF), vm(fine.shape, BF), vm((27, 8, 128), F32), vm((4, 8, 128), F32),
        dma((4,)),
        vm(fine.shape, BF), vm(w_down.shape, BF), vm(w_conv.shape, BF), vm(cotangent.shape, BF),
        vm((10, 18, 8, 128), BF), vm((10, 18, 8, 128), BF),
        vm((2, 8, 16, 1, 128), F32), vm((2, 8, 16, 1, 128), F32),
        vm((2, 10, 18, 1, 128), F32), vm((2, 10, 18, 1, 128), F32),
        vm((10, 144, 384), BF), vm((10, 128, 384), BF),
        vm((10, 144, 384), BF), vm((10, 128, 384), BF),
        vm((8, 16, 8, 128), BF),
        vm((128, 1024), BF), vm((512, 1024), BF),
        vm((1024, 128), F32), vm((1024, 128), BF),
        vm((32, 128, 128), BF),
        vm((4, 4, 128, 128), BF), vm((4, 4, 128, 128), BF),
        vm((4, 16, 32, 128), BF),
        vm((2, 4, 16, 128), BF), vm((2, 8, 16, 128), BF),
        vm((2, 16, 128), BF), vm((2, 8, 16, 128), BF),
        vm((6, 128, 384), F32), vm((512, 128), F32),
        pltpu.SMEM((1, 1, 2), jnp.int32),
        dma((5,)), dma, dma((2,)), dma((2,)),
        dma, dma((4,)), dma, dma((4,)), dma, dma((2,)), dma, dma((2,)),
    ]
    anym = pl.BlockSpec(memory_space=pl.ANY)
    out, d_fine, d_wconv, d_wdown = pl.pallas_call(
        kernel,
        out_shape=(
            jax.ShapeDtypeStruct(cotangent.shape, BF),
            jax.ShapeDtypeStruct(fine.shape, BF),
            jax.ShapeDtypeStruct((27, 8, 128), F32),
            jax.ShapeDtypeStruct((4, 8, 128), F32),
        ),
        in_specs=[anym, anym, anym, anym, anym],
        out_specs=(anym, anym, anym, anym),
        scratch_shapes=scratch,
        compiler_params=pltpu.CompilerParams(
            collective_id=0, has_side_effects=True, vmem_limit_bytes=56 * 1024 * 1024
        ),
    )(fine, jnp.transpose(occupied, (0, 2, 1)), w_down, w_conv, cotangent)
    out, d_fine, d_wconv, d_wdown = publish(out, d_fine, d_wconv, d_wdown)
    return out, d_fine.reshape(16, 32, 8, 128), d_wconv, d_wdown


def solution(mesh):
    in_specs = (P("gx", "gy", "gz", None), P("gx", "gy", "gz"), P(), P(), P("gx", "gy", "gz", None))
    out_specs = (
        P("gx", "gy", "gz", None),
        P("gx", "gy", "gz", None),
        P(None, "gx", None),
        P(None, "gx", None),
    )
    return jax.shard_map(body, mesh=mesh, in_specs=in_specs, out_specs=out_specs, check_vma=False)
```

time: 57.7 us -> 45.5 us (0.79)
  local copies, waits for them, and re-layouts: 7.91 us -> 0 us
  Pallas kernels: 48.9 us -> 44.7 us
    unnamed x15 -> x0, local copies, waits for them, and re-layouts: 7.91 us -> none
    pallas_call x1, Pallas kernels: 48.9 us -> 42.5 us  [body(): pl.pallas_call(kernel, out_shape=(jax.ShapeDtypeStruct(cotangent.shape, B...]
    pallas_call x0 -> x1, Pallas kernels: none -> 2.15 us  [publish(): pl.pallas_call(publish_kernel, out_shape=tuple((jax.ShapeDtypeStruct(a.sh...]
where the time goes in v2:
time: 45.5 us; the launch traced here: 45.3 us
  Pallas kernels  44.7 us (98%)
  between operations  0.64 us (1%)
    pallas_call x1, Pallas kernels, body(): pl.pallas_call(kernel, out_shape=(jax.ShapeDtypeStruct(cotangent.shape, B...  42.5 us
    pallas_call x1, Pallas kernels, publish(): pl.pallas_call(publish_kernel, out_shape=tuple((jax.ShapeDtypeStruct(a.sh...  2.15 us

profile of v2, /device:TPU:1, one launch (start us, length us, event | category | flops | bytes accessed | tf_op | source)
XLA Modules:
  0.0 45.3 jit_solution(2882677314185073901)
XLA Ops:
  0.6 42.5 %shard_map.84 = (bf16[8,16,8,128]{3,2,1,0:T(8,128)(2,1)}, bf16[8,2,16,2,8,128]{5,4,3,2,1,0:T(8,128)(2,1)}, f32[27,8,128]{2,1,0:T(8,128)}, f32[4,8,128]{2,1,0:T(8,128)}) custom-call(bf16[8,2,16,2,8,128]{5,4,3,2,1,0:T(8,128)(2,1)} %bitcast.3, s32[1,1,2]{2,1,0:T(1,128)} %bitcast.4, bf16[4,128,128]{2,1,0:T(8,128)(2,1)} %w_down.1, bf16[27,128,128]{2,1,0:T(8,128)(2,1)} %w_conv.1, ...), custom_call_target="tpu_custom_call" | custom-call | tf_op jit(solution)/shard_map/pallas_call | solution.py:451
  43.2 2.1 %shard_map.85 = (bf16[8,16,8,128]{3,2,1,0:T(8,128)(2,1)}, bf16[8,2,16,2,8,128]{5,4,3,2,1,0:T(8,128)(2,1)}, f32[27,8,128]{2,1,0:T(8,128)}, f32[4,8,128]{2,1,0:T(8,128)}) custom-call(bf16[8,16,8,128]{3,2,1,0:T(8,128)(2,1)} %get-tuple-element.12.refs_0_, bf16[8,2,16,2,8,128]{5,4,3,2,1,0:T(8,128)(2,1)} %get-tuple-element.13.refs_1_, ...), custom_call_target="tpu_custom_call" | custom-call | tf_op jit(solution)/shard_map/pallas_call | solution.py:413

commit v3 on v2

--- a/solution.py
+++ b/solution.py
@@ -12,12 +12,12 @@
 NGX, NGY, NGZ = 16, 4, 4
 NEIGHBOURS = [
     (sx, sy, sz)
-    for sx in (-1, 1, 0)
+    for sx in (0, -1, 1)
     for sz in (-1, 1, 0)
     for sy in (-1, 1, 0)
     if (sx, sy, sz) != (0, 0, 0)
 ]
-FAR = 18
+NEAR = 8
 GROUPS = [3, 4, 5, 0, 1, 2, 6, 7, 8]
 SLOTS = [3 * g + 2 - b for g in GROUPS for b in range(3)] + [27, 28, 29, 30]
 
@@ -28,8 +28,8 @@
 
 def kernel(
     fine, occupied, w_down, w_conv, cot,
-    out_h, d_fine_h, d_wconv_h, d_wdown_h,
-    out, d_fine, d_wconv, d_wdown, store_sem, fine_v, wd_v, wc_v, cot_v,
+    out, d_fine, d_wconv, d_wdown,
+    fine_v, wd_v, wc_v, cot_v,
     mp, ap, mz, az, mzr, azr, me_v, mo_v, ae_v, ao_v,
     zv, act_t, patch_t, acc, dz_v, grads,
     r0, p1, r1, p2, r3, p3, r4, gsum, dsum,
@@ -121,7 +121,7 @@
                 dst = zr.at[(1 - sz) // 2, dxs, dys]
             copies.append(
                 pltpu.make_async_remote_copy(
-                    src_ref=src, dst_ref=dst, send_sem=halo_s, recv_sem=rs.at[0 if i < FAR else 1],
+                    src_ref=src, dst_ref=dst, send_sem=halo_s, recv_sem=rs.at[1 if i < NEAR else 0],
                     device_id=near((sx, sy, sz)), device_id_type=MESH,
                 )
             )
@@ -147,7 +147,6 @@
     ap[1:9, 1:17] = act.astype(BF)
     az[0] = act[:, :, 0:1, :]
     az[1] = act[:, :, 7:8, :]
-    halo(ap, az, azr, ah_r)
     act_t[...] = act.reshape(1024, 128).T.astype(BF)
     for i in range(4):
         patch_t[i * 128 : (i + 1) * 128] = patches[i].T
@@ -312,6 +311,7 @@
     dsum[...] = dot(patch_t[:, 128:896], dz_v[128:896], 1, 0)
 
     landed(mh_r.at[0], far_bytes)
+    halo(ap, az, azr, ah_r)
     build(mp, mzr, me_v, mo_v, 0, 1)
     build(mp, mzr, me_v, mo_v, 9, 10)
     for i in range(3, 9):
@@ -343,16 +343,12 @@
             i = 2 * a + b
             d_fine[:, a, :, b] = d[:, i * 128 : (i + 1) * 128].reshape(8, 16, 8, 128).astype(BF)
 
-    def store(i):
-        pairs = ((out, out_h), (d_fine, d_fine_h), (d_wconv, d_wconv_h), (d_wdown, d_wdown_h))
-        return pltpu.make_async_copy(*pairs[i], store_sem.at[i])
-
-    store(1).start()
+    s3_start(0)
+    s3_start(1)
 
     landed(ah_r.at[0], far_bytes)
     landed(ah_r.at[1], near_bytes)
     build(ap, azr, ae_v, ao_v, 0, 10)
-    s3_start(0)
     for g in range(0, 9, 2):
         pair = [g, g + 1] if g < 8 else [8]
         left = jnp.concatenate([cut(ae_v, ao_v, h // 3, 8, h % 3) for h in pair], axis=1)
@@ -364,14 +360,10 @@
     out[...] = (
         zv[...].astype(F32) + occ[None] * acc[...].reshape(8, 16, 8, 128)
     ).astype(BF)
-    store(0).start()
-    s3_start(1)
     s4_start(0)
     s4_start(1)
     s4_finish(0)
     s4_finish(1)
-    store(2).start()
-    store(3).start()
 
     landed(halo_s, acc.at[0:568])
     landed(halo_s, acc.at[0:568])
@@ -379,46 +371,25 @@
     landed(s1_s, r1.at[:, pl.ds(1, 15)])
     landed(s3_s, r3.at[:, pl.ds(1, 7)])
     landed(s4_s, r4.at[:, pl.ds(1, 7)])
-    for i in range(4):
-        store(i).wait()
-
-
-PARTS = (1, 4, 1, 1)
 
 
 def publish_kernel(*refs):
-    ins, outs, held = refs[:4], refs[4:8], refs[8:12]
-    load_sem, store_sem = refs[12:]
-    pieces = []
-    for i, parts in enumerate(PARTS):
-        size = ins[i].shape[0] // parts
-        for p in range(parts):
-            at = pl.ds(p * size, size)
-            k = len(pieces)
-            pieces.append((
-                pltpu.make_async_copy(ins[i].at[at], held[i].at[at], load_sem.at[k]),
-                pltpu.make_async_copy(held[i].at[at], outs[i].at[at], store_sem.at[k]),
-            ))
-    for load, _ in pieces:
-        load.start()
-    for load, store in pieces:
-        load.wait()
-        store.start()
-    for _, store in pieces:
-        store.wait()
+    ins, outs, sem = refs[:4], refs[4:8], refs[8]
+    copies = [pltpu.make_async_copy(ins[i], outs[i], sem.at[i]) for i in range(4)]
+    for c in copies:
+        c.start()
+    for c in copies:
+        c.wait()
 
 
 def publish(*arrays):
-    anym = pl.BlockSpec(memory_space=pl.ANY)
     return pl.pallas_call(
         publish_kernel,
         out_shape=tuple(jax.ShapeDtypeStruct(a.shape, a.dtype) for a in arrays),
-        in_specs=[anym] * 4,
-        out_specs=(anym,) * 4,
-        scratch_shapes=[pltpu.VMEM(a.shape, a.dtype) for a in arrays]
-        + [pltpu.SemaphoreType.DMA((sum(PARTS),))] * 2,
-        compiler_params=pltpu.CompilerParams(vmem_limit_bytes=56 * 1024 * 1024),
-    )(*arrays)
+        in_specs=[pl.BlockSpec(memory_space=pltpu.VMEM)] * 4,
+        out_specs=(pl.BlockSpec(memory_space=pl.ANY),) * 4,
+        scratch_shapes=[pltpu.SemaphoreType.DMA((4,))],
+    )(*[pltpu.with_memory_space_constraint(a, pltpu.VMEM) for a in arrays])
 
 
 def body(fine, occupied, w_down, w_conv, cotangent):
@@ -426,8 +397,6 @@
     vm = pltpu.VMEM
     dma = pltpu.SemaphoreType.DMA
     scratch = [
-        vm(cotangent.shape, BF), vm(fine.shape, BF), vm((27, 8, 128), F32), vm((4, 8, 128), F32),
-        dma((4,)),
         vm(fine.shape, BF), vm(w_down.shape, BF), vm(w_conv.shape, BF), vm(cotangent.shape, BF),
         vm((10, 18, 8, 128), BF), vm((10, 18, 8, 128), BF),
         vm((2, 8, 16, 1, 128), F32), vm((2, 8, 16, 1, 128), F32),
@@ -448,16 +417,15 @@
         dma, dma((4,)), dma, dma((4,)), dma, dma((2,)), dma, dma((2,)),
     ]
     anym = pl.BlockSpec(memory_space=pl.ANY)
+    vmem = pl.BlockSpec(memory_space=pltpu.VMEM)
     out, d_fine, d_wconv, d_wdown = pl.pallas_call(
         kernel,
         out_shape=(
-            jax.ShapeDtypeStruct(cotangent.shape, BF),
-            jax.ShapeDtypeStruct(fine.shape, BF),
-            jax.ShapeDtypeStruct((27, 8, 128), F32),
-            jax.ShapeDtypeStruct((4, 8, 128), F32),
+            vm(cotangent.shape, BF), vm(fine.shape, BF),
+            vm((27, 8, 128), F32), vm((4, 8, 128), F32),
         ),
         in_specs=[anym, anym, anym, anym, anym],
-        out_specs=(anym, anym, anym, anym),
+        out_specs=(vmem, vmem, vmem, vmem),
         scratch_shapes=scratch,
         compiler_params=pltpu.CompilerParams(
             collective_id=0, has_side_effects=True, vmem_limit_bytes=56 * 1024 * 1024

time: 45.5 us -> 41.6 us (0.914)
  Pallas kernels: 44.7 us -> 40.9 us
    pallas_call x1, Pallas kernels: 42.5 us -> 39.8 us  [body(): pl.pallas_call(kernel, out_shape=(vm(cotangent.shape, BF), vm(fine.shape,...]
    pallas_call x1, Pallas kernels: 2.15 us -> 1.12 us  [publish(): pl.pallas_call(publish_kernel, out_shape=tuple((jax.ShapeDtypeStruct(a.sh...]
where the time goes in v3:
time: 41.6 us; the launch traced here: 41.5 us
  Pallas kernels  40.9 us (98%)
  between operations  0.64 us (2%)
    pallas_call x1, Pallas kernels, body(): pl.pallas_call(kernel, out_shape=(vm(cotangent.shape, BF), vm(fine.shape,...  39.8 us
    pallas_call x1, Pallas kernels, publish(): pl.pallas_call(publish_kernel, out_shape=tuple((jax.ShapeDtypeStruct(a.sh...  1.12 us

profile of v3, /device:TPU:1, one launch (start us, length us, event | category | flops | bytes accessed | tf_op | source)
XLA Modules:
  0.0 41.5 jit_solution(7858270256472924948)
XLA Ops:
  0.6 39.8 %shard_map.84 = (bf16[8,16,8,128]{3,2,1,0:T(8,128)(2,1)S(1)}, bf16[8,2,16,2,8,128]{5,4,3,2,1,0:T(8,128)(2,1)S(1)}, f32[27,8,128]{2,1,0:T(8,128)S(1)}, f32[4,8,128]{2,1,0:T(8,128)S(1)}) custom-call(bf16[8,2,16,2,8,128]{5,4,3,2,1,0:T(8,128)(2,1)} %bitcast.3, s32[1,1,2]{2,1,0:T(1,128)} %bitcast.4, bf16[4,128,128]{2,1,0:T(8,128)(2,1)} %w_down.1, ...), custom_call_target="tpu_custom_call" | custom-call | tf_op jit(solution)/shard_map/pallas_call | solution.py:421
  40.4 1.1 %shard_map.85 = (bf16[8,16,8,128]{3,2,1,0:T(8,128)(2,1)}, bf16[8,2,16,2,8,128]{5,4,3,2,1,0:T(8,128)(2,1)}, f32[27,8,128]{2,1,0:T(8,128)}, f32[4,8,128]{2,1,0:T(8,128)}) custom-call(bf16[8,16,8,128]{3,2,1,0:T(8,128)(2,1)S(1)} %get-tuple-element.12.refs_0_, bf16[8,2,16,2,8,128]{5,4,3,2,1,0:T(8,128)(2,1)S(1)} %get-tuple-element.13.refs_1_, ...), custom_call_target="tpu_custom_call" | custom-call | tf_op jit(solution)/shard_map/pallas_call | solution.py:386

commit v4 on v3

--- a/solution.py
+++ b/solution.py
@@ -15,7 +15,7 @@
     for sx in (0, -1, 1)
     for sz in (-1, 1, 0)
     for sy in (-1, 1, 0)
-    if (sx, sy, sz) != (0, 0, 0)
+    if abs(sx) + abs(sy) + abs(sz) in (1, 2)
 ]
 NEAR = 8
 GROUPS = [3, 4, 5, 0, 1, 2, 6, 7, 8]
@@ -30,7 +30,7 @@
     fine, occupied, w_down, w_conv, cot,
     out, d_fine, d_wconv, d_wdown,
     fine_v, wd_v, wc_v, cot_v,
-    mp, ap, mz, az, mzr, azr, me_v, mo_v, ae_v, ao_v,
+    mp, ap, mz, az, mze, aze, mzr, azr, mzer, azer, me_v, mo_v, ae_v, ao_v,
     zv, act_t, patch_t, acc, dz_v, grads,
     r0, p1, r1, p2, r3, p3, r4, gsum, dsum,
     occ_v, load_sem, halo_s, mh_r, ah_r, s0_s, s0_r, s1_s, s1_r, s3_s, s3_r, s4_s, s4_r,
@@ -100,40 +100,49 @@
     def _(x):
         m = cot_v[x].astype(F32) * occ
         mp[x + 1, 1:17] = m.astype(BF)
-        mz[0, x] = m[:, 0:1, :]
-        mz[1, x] = m[:, 7:8, :]
-
-    pl.semaphore_wait(barrier, 26 + 1 + 15 + 7 + 7)
-
-    def halo(pad, zs, zr, rs):
-        copies = []
+        for side, k in ((0, 0), (1, 7)):
+            mz[side, x] = m[:, k, :].astype(BF)
+            mze[side, x, 0] = m[0, k : k + 1]
+            mze[side, x, 1] = m[15, k : k + 1]
+
+    pl.semaphore_wait(barrier, 18 + 1 + 15 + 7 + 7)
+
+    def send(src, dst, sem, s):
+        pltpu.make_async_remote_copy(
+            src_ref=src, dst_ref=dst, send_sem=halo_s, recv_sem=sem,
+            device_id=near(s), device_id_type=MESH,
+        ).start()
+
+    def halo(pad, zs, zse, zr, zer, rs):
         for i, (sx, sy, sz) in enumerate(NEIGHBOURS):
             sxs = {-1: slice(1, 2), 0: slice(1, 9), 1: slice(8, 9)}[sx]
             dxs = {-1: slice(9, 10), 0: slice(1, 9), 1: slice(0, 1)}[sx]
             sys_ = {-1: slice(1, 2), 0: slice(1, 17), 1: slice(16, 17)}[sy]
             dys = {-1: slice(17, 18), 0: slice(1, 17), 1: slice(0, 1)}[sy]
+            up, down = (sz + 1) // 2, (1 - sz) // 2
+            zxs = slice(sxs.start - 1, sxs.stop - 1)
             if sz == 0:
-                src = pad.at[sxs, sys_]
-                dst = pad.at[dxs, dys]
+                src, dst = pad.at[sxs, sys_], pad.at[dxs, dys]
+            elif sy == 0:
+                src, dst = zs.at[up, zxs], zr.at[down, dxs]
             else:
-                src = zs.at[(sz + 1) // 2, slice(sxs.start - 1, sxs.stop - 1),
-                            slice(sys_.start - 1, sys_.stop - 1)]
-                dst = zr.at[(1 - sz) // 2, dxs, dys]
-            copies.append(
-                pltpu.make_async_remote_copy(
-                    src_ref=src, dst_ref=dst, send_sem=halo_s, recv_sem=rs.at[1 if i < NEAR else 0],
-                    device_id=near((sx, sy, sz)), device_id_type=MESH,
-                )
-            )
-        for c in copies:
-            c.start()
+                src = zse.at[up, zxs, (sy + 1) // 2]
+                dst = zer.at[down, dxs, (1 - sy) // 2]
+            send(src, dst, rs.at[1 if i < NEAR else 0], (sx, sy, sz))
+
+    def corners(zer, rs):
+        for sx in (-1, 1):
+            for side in range(2):
+                src = zer.at[side, 1 if sx < 0 else 8]
+                dst = zer.at[side, 9 if sx < 0 else 0]
+                send(src, dst, rs.at[0], (sx, 0, 0))
 
     def landed(sem, ref):
         pltpu.make_async_copy(ref, ref, sem).wait()
 
-    far_bytes, near_bytes = acc.at[0:216], acc.at[0:352]
-
-    halo(mp, mz, mzr, mh_r)
+    far_bytes, near_bytes = acc.at[0:184], acc.at[0:224]
+
+    halo(mp, mz, mze, mzr, mzer, mh_r)
 
     loads[1].wait()
     loads[2].wait()
@@ -145,8 +154,10 @@
     act = jnp.maximum(zval.astype(F32), 0.0)
     zv[...] = zval
     ap[1:9, 1:17] = act.astype(BF)
-    az[0] = act[:, :, 0:1, :]
-    az[1] = act[:, :, 7:8, :]
+    for side, k in ((0, 0), (1, 7)):
+        az[side] = act[:, :, k, :].astype(BF)
+        aze[side, :, 0] = act[:, 0, k : k + 1]
+        aze[side, :, 1] = act[:, 15, k : k + 1]
     act_t[...] = act.reshape(1024, 128).T.astype(BF)
     for i in range(4):
         patch_t[i * 128 : (i + 1) * 128] = patches[i].T
@@ -157,7 +168,7 @@
         jnp.logical_or(yi > 0, gy > 0), jnp.logical_or(yi < 17, gy < NGY - 1)
     )
 
-    def build(pad, zr, even, odd, first, last):
+    def build(pad, zr, zer, even, odd, first, last):
         @pl.loop(first, last)
         def _(x):
             inside_x = jnp.logical_and(
@@ -167,8 +178,14 @@
             low = jnp.where(gz > 0, 1.0, 0.0)
             high = jnp.where(gz < NGZ - 1, 1.0, 0.0)
             m = pad[x].astype(F32)
-            lo = jnp.where(kk == 0, zr[0, x] * low, pltpu.roll(m, 1, 1)) * keep
-            hi = jnp.where(kk == 7, zr[1, x] * high, pltpu.roll(m, 7, 1)) * keep
+            face = [
+                jnp.concatenate(
+                    [zer[d, x, 0:1], zr[d, x].astype(F32)[:, None, :], zer[d, x, 1:2]], axis=0
+                )
+                for d in range(2)
+            ]
+            lo = jnp.where(kk == 0, face[0] * low, pltpu.roll(m, 1, 1)) * keep
+            hi = jnp.where(kk == 7, face[1] * high, pltpu.roll(m, 7, 1)) * keep
             for b, v in enumerate((lo, m * keep, hi)):
                 even[x, :, b * 128 : (b + 1) * 128] = v.reshape(144, 128).astype(BF)
                 odd[x, :, b * 128 : (b + 1) * 128] = v[1:17].reshape(128, 128).astype(BF)
@@ -197,6 +214,19 @@
             [wc_v[9 * dx + 3 * dy + 2 - b] for dy in range(3) for b in range(3)], axis=1
         )
         return slice(mine * 128, (mine + count) * 128), dot(left, right, 1, 1)
+
+    def back_own():
+        left = jnp.concatenate([cut(me_v, mo_v, 1, 8, 2 - dy) for dy in range(3)], axis=1)
+        right = [
+            jnp.concatenate(
+                [wc_v[9 * dx + 3 * dy + 2 - b] for dy in range(3) for b in range(3)], axis=1
+            )
+            for dx in range(3)
+        ]
+        both = dot(left, jnp.concatenate(right[:2], axis=0), 1, 1)
+        acc[...] = both[:, 128:]
+        acc[:896] += both[128:, :128]
+        acc[128:] += dot(left[:896], right[2], 1, 1)
 
     def dz_of(first, last):
         d_act = acc[first * 128 : last * 128].reshape(last - first, 16, 8, 128)
@@ -295,47 +325,41 @@
             grads[3 * i + b] = d[:, b * 128 : (b + 1) * 128].astype(BF)
 
     landed(mh_r.at[1], near_bytes)
-    build(mp, mzr, me_v, mo_v, 1, 9)
+    corners(mzer, mh_r)
+    halo(ap, az, aze, azr, azer, ah_r)
+    build(mp, mzr, mzer, me_v, mo_v, 1, 9)
     for i in range(3):
         put(i, conv_grad(GROUPS[i], own))
     s0(0).start()
     loads[3].wait()
-    acc[...] = back(1, own)[1]
     s0_finish(0)
     for i in range(3, 9):
         gsum[i - 3] = conv_grad(GROUPS[i], own)
-    for dx in (0, 2):
-        where, d = back(dx, own)
-        acc[where] += d
-    dz_of(1, 7)
-    dsum[...] = dot(patch_t[:, 128:896], dz_v[128:896], 1, 0)
 
     landed(mh_r.at[0], far_bytes)
-    halo(ap, az, azr, ah_r)
-    build(mp, mzr, me_v, mo_v, 0, 1)
-    build(mp, mzr, me_v, mo_v, 9, 10)
+    build(mp, mzr, mzer, me_v, mo_v, 0, 1)
+    build(mp, mzr, mzer, me_v, mo_v, 9, 10)
     for i in range(3, 9):
         put(i, gsum[i - 3] + conv_grad(GROUPS[i], edge))
         if i == 5:
             s0(1).start()
         if i == 7:
             s0(2).start()
+    back_own()
     for dx in (0, 2):
         where, d = back(dx, edge)
         acc[where] += d
-    dz_of(0, 1)
-    dz_of(7, 8)
-    d = dsum[...] + dot(
-        jnp.concatenate([patch_t[:, :128], patch_t[:, 896:]], axis=1),
-        jnp.concatenate([dz_v[:128], dz_v[896:]], axis=0), 1, 0,
-    )
+    dz_of(0, 8)
+    s0_finish(1)
+    d = dot(patch_t[...], dz_v[...], 1, 0)
     for i in range(4):
         grads[27 + i] = d[i * 128 : (i + 1) * 128].astype(BF)
     grads[31] = jnp.zeros((128, 128), BF)
     s0(3).start()
-    s0_finish(1)
     s0_finish(2)
     s0_finish(3)
+    landed(ah_r.at[1], near_bytes)
+    corners(azer, ah_r)
 
     d = dot(dz_v[...], wd_v[...].reshape(512, 128), 1, 1)
     for a in range(2):
@@ -347,8 +371,7 @@
     s3_start(1)
 
     landed(ah_r.at[0], far_bytes)
-    landed(ah_r.at[1], near_bytes)
-    build(ap, azr, ae_v, ao_v, 0, 10)
+    build(ap, azr, azer, ae_v, ao_v, 0, 10)
     for g in range(0, 9, 2):
         pair = [g, g + 1] if g < 8 else [8]
         left = jnp.concatenate([cut(ae_v, ao_v, h // 3, 8, h % 3) for h in pair], axis=1)
@@ -365,8 +388,8 @@
     s4_finish(0)
     s4_finish(1)
 
-    landed(halo_s, acc.at[0:568])
-    landed(halo_s, acc.at[0:568])
+    landed(halo_s, acc.at[0:408])
+    landed(halo_s, acc.at[0:408])
     landed(s0_s, r0)
     landed(s1_s, r1.at[:, pl.ds(1, 15)])
     landed(s3_s, r3.at[:, pl.ds(1, 7)])
@@ -399,8 +422,10 @@
     scratch = [
         vm(fine.shape, BF), vm(w_down.shape, BF), vm(w_conv.shape, BF), vm(cotangent.shape, BF),
         vm((10, 18, 8, 128), BF), vm((10, 18, 8, 128), BF),
-        vm((2, 8, 16, 1, 128), F32), vm((2, 8, 16, 1, 128), F32),
-        vm((2, 10, 18, 1, 128), F32), vm((2, 10, 18, 1, 128), F32),
+        vm((2, 8, 16, 128), BF), vm((2, 8, 16, 128), BF),
+        vm((2, 8, 2, 1, 128), F32), vm((2, 8, 2, 1, 128), F32),
+        vm((2, 10, 16, 128), BF), vm((2, 10, 16, 128), BF),
+        vm((2, 10, 2, 1, 128), F32), vm((2, 10, 2, 1, 128), F32),
         vm((10, 144, 384), BF), vm((10, 128, 384), BF),
         vm((10, 144, 384), BF), vm((10, 128, 384), BF),
         vm((8, 16, 8, 128), BF),

time: 41.6 us -> 39.3 us (0.945)
  Pallas kernels: 40.9 us -> 38.6 us
    pallas_call x1, Pallas kernels: 39.8 us -> 37.5 us  [body(): pl.pallas_call(kernel, out_shape=(vm(cotangent.shape, BF), vm(fine.shape,...]
where the time goes in v4:
time: 39.3 us; the launch traced here: 39.2 us
  Pallas kernels  38.6 us (98%)
  between operations  0.64 us (2%)
    pallas_call x1, Pallas kernels, body(): pl.pallas_call(kernel, out_shape=(vm(cotangent.shape, BF), vm(fine.shape,...  37.5 us
    pallas_call x1, Pallas kernels, publish(): pl.pallas_call(publish_kernel, out_shape=tuple((jax.ShapeDtypeStruct(a.sh...  1.12 us

profile of v4, /device:TPU:1, one launch (start us, length us, event | category | flops | bytes accessed | tf_op | source)
XLA Modules:
  0.0 39.2 jit_solution(3998004014553245009)
XLA Ops:
  0.6 37.5 %shard_map.84 = (bf16[8,16,8,128]{3,2,1,0:T(8,128)(2,1)S(1)}, bf16[8,2,16,2,8,128]{5,4,3,2,1,0:T(8,128)(2,1)S(1)}, f32[27,8,128]{2,1,0:T(8,128)S(1)}, f32[4,8,128]{2,1,0:T(8,128)S(1)}) custom-call(bf16[8,2,16,2,8,128]{5,4,3,2,1,0:T(8,128)(2,1)} %bitcast.3, s32[1,1,2]{2,1,0:T(1,128)} %bitcast.4, bf16[4,128,128]{2,1,0:T(8,128)(2,1)} %w_down.1, ...), custom_call_target="tpu_custom_call" | custom-call | tf_op jit(solution)/shard_map/pallas_call | solution.py:446
  38.1 1.1 %shard_map.85 = (bf16[8,16,8,128]{3,2,1,0:T(8,128)(2,1)}, bf16[8,2,16,2,8,128]{5,4,3,2,1,0:T(8,128)(2,1)}, f32[27,8,128]{2,1,0:T(8,128)}, f32[4,8,128]{2,1,0:T(8,128)}) custom-call(bf16[8,16,8,128]{3,2,1,0:T(8,128)(2,1)S(1)} %get-tuple-element.12.refs_0_, bf16[8,2,16,2,8,128]{5,4,3,2,1,0:T(8,128)(2,1)S(1)} %get-tuple-element.13.refs_1_, ...), custom_call_target="tpu_custom_call" | custom-call | tf_op jit(solution)/shard_map/pallas_call | solution.py:409

commit v5 on v4

--- a/solution.py
+++ b/solution.py
@@ -8,6 +8,7 @@
 BF = jnp.bfloat16
 F32 = jnp.float32
 MESH = pl.DeviceIdType.MESH
+REST = [(dy, b) for dy in range(3) for b in range(3) if (dy, b) != (1, 1)]
 
 NGX, NGY, NGZ = 16, 4, 4
 NEIGHBOURS = [
@@ -32,7 +33,7 @@
     fine_v, wd_v, wc_v, cot_v,
     mp, ap, mz, az, mze, aze, mzr, azr, mzer, azer, me_v, mo_v, ae_v, ao_v,
     zv, act_t, patch_t, acc, dz_v, grads,
-    r0, p1, r1, p2, r3, p3, r4, gsum, dsum,
+    r0, p1, r1, p2, r3, p3, r4, gsum, centre,
     occ_v, load_sem, halo_s, mh_r, ah_r, s0_s, s0_r, s1_s, s1_r, s3_s, s3_r, s4_s, s4_r,
 ):
     gx, gy, gz = lax.axis_index("gx"), lax.axis_index("gy"), lax.axis_index("gz")
@@ -198,11 +199,14 @@
     own = {0: (2, 0, 7), 1: (1, 0, 8), 2: (1, 1, 7)}
     edge = {0: (9, 7, 1), 2: (0, 0, 1)}
 
-    def conv_grad(g, where):
-        first, mine, count = where[g // 3]
+    def conv_grad(dx, where):
+        first, mine, count = where[dx]
+        if where is own:
+            right = rest(first, count)
+        else:
+            right = [cut(me_v, mo_v, first, count, 2 - dy) for dy in range(3)]
         return dot(
-            act_t[:, mine * 128 : (mine + count) * 128],
-            cut(me_v, mo_v, first, count, 2 - g % 3), 1, 0,
+            act_t[:, mine * 128 : (mine + count) * 128], jnp.concatenate(right, axis=1), 1, 0
         )
 
     def back(dx, where):
@@ -215,16 +219,22 @@
         )
         return slice(mine * 128, (mine + count) * 128), dot(left, right, 1, 1)
 
+    def rest(first, count):
+        return [
+            cut(me_v, mo_v, first, count, 2),
+            mo_v[first : first + count, :, :128].reshape(count * 128, 128),
+            mo_v[first : first + count, :, 256:].reshape(count * 128, 128),
+            cut(me_v, mo_v, first, count, 0),
+        ]
+
     def back_own():
-        left = jnp.concatenate([cut(me_v, mo_v, 1, 8, 2 - dy) for dy in range(3)], axis=1)
+        left = jnp.concatenate(rest(1, 8), axis=1)
         right = [
-            jnp.concatenate(
-                [wc_v[9 * dx + 3 * dy + 2 - b] for dy in range(3) for b in range(3)], axis=1
-            )
+            jnp.concatenate([wc_v[9 * dx + 3 * dy + 2 - b] for dy, b in REST], axis=1)
             for dx in range(3)
         ]
         both = dot(left, jnp.concatenate(right[:2], axis=0), 1, 1)
-        acc[...] = both[:, 128:]
+        acc[...] += both[:, 128:]
         acc[:896] += both[128:, :128]
         acc[128:] += dot(left[:896], right[2], 1, 1)
 
@@ -320,32 +330,45 @@
                     else:
                         d_wdown[tap - 27] = v[8 * h : 8 * h + 8]
 
-    def put(i, d):
-        for b in range(3):
-            grads[3 * i + b] = d[:, b * 128 : (b + 1) * 128].astype(BF)
+    def put(i, d, middle=None):
+        parts = [d[:, b : b + 128] for b in range(0, d.shape[1], 128)]
+        if middle is not None:
+            parts.insert(4, middle)
+        for b in range(9):
+            grads[9 * i + b] = parts[b].astype(BF)
+
+    loads[3].wait()
+    local = mp[1:9, 1:17].reshape(1024, 128)
+    both = dot(local, jnp.concatenate([wc_v[4], wc_v[13]], axis=0), 1, 1)
+    acc[...] = both[:, 128:]
+    acc[:896] += both[128:, :128]
+    acc[128:] += dot(local[:896], wc_v[22], 1, 1)
+    centre[0] = dot(act_t[:, :896], local[128:], 1, 0)
+    centre[1] = dot(act_t[...], local, 1, 0)
+    centre[2] = dot(act_t[:, 128:], local[:896], 1, 0)
 
     landed(mh_r.at[1], near_bytes)
     corners(mzer, mh_r)
     halo(ap, az, aze, azr, azer, ah_r)
     build(mp, mzr, mzer, me_v, mo_v, 1, 9)
-    for i in range(3):
-        put(i, conv_grad(GROUPS[i], own))
+    put(0, conv_grad(1, own), centre[1])
     s0(0).start()
-    loads[3].wait()
+    for i, dx in enumerate((0, 2)):
+        d = conv_grad(dx, own)
+        gsum[i, :, :512] = d[:, :512]
+        gsum[i, :, 512:640] = centre[dx]
+        gsum[i, :, 640:] = d[:, 512:]
+
     s0_finish(0)
-    for i in range(3, 9):
-        gsum[i - 3] = conv_grad(GROUPS[i], own)
+    back_own()
 
     landed(mh_r.at[0], far_bytes)
     build(mp, mzr, mzer, me_v, mo_v, 0, 1)
     build(mp, mzr, mzer, me_v, mo_v, 9, 10)
-    for i in range(3, 9):
-        put(i, gsum[i - 3] + conv_grad(GROUPS[i], edge))
-        if i == 5:
-            s0(1).start()
-        if i == 7:
-            s0(2).start()
-    back_own()
+    put(1, gsum[0] + conv_grad(0, edge))
+    s0(1).start()
+    put(2, gsum[1] + conv_grad(2, edge))
+    s0(2).start()
     for dx in (0, 2):
         where, d = back(dx, edge)
         acc[where] += d
@@ -436,7 +459,7 @@
         vm((4, 16, 32, 128), BF),
         vm((2, 4, 16, 128), BF), vm((2, 8, 16, 128), BF),
         vm((2, 16, 128), BF), vm((2, 8, 16, 128), BF),
-        vm((6, 128, 384), F32), vm((512, 128), F32),
+        vm((2, 128, 1152), F32), vm((3, 128, 128), F32),
         pltpu.SMEM((1, 1, 2), jnp.int32),
         dma((5,)), dma, dma((2,)), dma((2,)),
         dma, dma((4,)), dma, dma((4,)), dma, dma((2,)), dma, dma((2,)),

time: 39.3 us -> 38.7 us (0.985)
  Pallas kernels: 38.6 us -> 37.9 us
    pallas_call x1, Pallas kernels: 37.5 us -> 36.8 us  [body(): pl.pallas_call(kernel, out_shape=(vm(cotangent.shape, BF), vm(fine.shape,...]
where the time goes in v5:
time: 38.7 us; the launch traced here: 38.6 us
  Pallas kernels  37.9 us (98%)
  between operations  0.64 us (2%)
    pallas_call x1, Pallas kernels, body(): pl.pallas_call(kernel, out_shape=(vm(cotangent.shape, BF), vm(fine.shape,...  36.8 us
    pallas_call x1, Pallas kernels, publish(): pl.pallas_call(publish_kernel, out_shape=tuple((jax.ShapeDtypeStruct(a.sh...  1.12 us

profile of v5, /device:TPU:1, one launch (start us, length us, event | category | flops | bytes accessed | tf_op | source)
XLA Modules:
  0.0 38.6 jit_solution(13468510741756204785)
XLA Ops:
  0.6 36.8 %shard_map.84 = (bf16[8,16,8,128]{3,2,1,0:T(8,128)(2,1)S(1)}, bf16[8,2,16,2,8,128]{5,4,3,2,1,0:T(8,128)(2,1)S(1)}, f32[27,8,128]{2,1,0:T(8,128)S(1)}, f32[4,8,128]{2,1,0:T(8,128)S(1)}) custom-call(bf16[8,2,16,2,8,128]{5,4,3,2,1,0:T(8,128)(2,1)} %bitcast.3, s32[1,1,2]{2,1,0:T(1,128)} %bitcast.4, bf16[4,128,128]{2,1,0:T(8,128)(2,1)} %w_down.1, ...), custom_call_target="tpu_custom_call" | custom-call | tf_op jit(solution)/shard_map/pallas_call | solution.py:469
  37.5 1.1 %shard_map.85 = (bf16[8,16,8,128]{3,2,1,0:T(8,128)(2,1)}, bf16[8,2,16,2,8,128]{5,4,3,2,1,0:T(8,128)(2,1)}, f32[27,8,128]{2,1,0:T(8,128)}, f32[4,8,128]{2,1,0:T(8,128)}) custom-call(bf16[8,16,8,128]{3,2,1,0:T(8,128)(2,1)S(1)} %get-tuple-element.12.refs_0_, bf16[8,2,16,2,8,128]{5,4,3,2,1,0:T(8,128)(2,1)S(1)} %get-tuple-element.13.refs_1_, ...), custom_call_target="tpu_custom_call" | custom-call | tf_op jit(solution)/shard_map/pallas_call | solution.py:432

commit v6 on v5

--- a/solution.py
+++ b/solution.py
@@ -264,7 +264,7 @@
 
         @pl.loop(1, 16)
         def _(n):
-            s1(j, n).start()
+            s1(j, lax.rem(n + 8, 15) + 1).start()
 
     def s1_finish(j):
         landed(s1_r.at[j], r1.at[j, pl.ds(1, 15)])

time: 38.7 us -> 39.1 us (1.010)
  Pallas kernels: 37.9 us -> 38.3 us
    pallas_call x1, Pallas kernels: 36.8 us -> 37.2 us  [body(): pl.pallas_call(kernel, out_shape=(vm(cotangent.shape, BF), vm(fine.shape,...]
where the time goes in v6:
time: 39.1 us; the launch traced here: 39 us
  Pallas kernels  38.3 us (98%)
  between operations  0.64 us (2%)
    pallas_call x1, Pallas kernels, body(): pl.pallas_call(kernel, out_shape=(vm(cotangent.shape, BF), vm(fine.shape,...  37.2 us
    pallas_call x1, Pallas kernels, publish(): pl.pallas_call(publish_kernel, out_shape=tuple((jax.ShapeDtypeStruct(a.sh...  1.12 us

profile of v6, /device:TPU:1, one launch (start us, length us, event | category | flops | bytes accessed | tf_op | source)
XLA Modules:
  0.0 39.0 jit_solution(14751214697043878994)
XLA Ops:
  0.6 37.2 %shard_map.84 = (bf16[8,16,8,128]{3,2,1,0:T(8,128)(2,1)S(1)}, bf16[8,2,16,2,8,128]{5,4,3,2,1,0:T(8,128)(2,1)S(1)}, f32[27,8,128]{2,1,0:T(8,128)S(1)}, f32[4,8,128]{2,1,0:T(8,128)S(1)}) custom-call(bf16[8,2,16,2,8,128]{5,4,3,2,1,0:T(8,128)(2,1)} %bitcast.3, s32[1,1,2]{2,1,0:T(1,128)} %bitcast.4, bf16[4,128,128]{2,1,0:T(8,128)(2,1)} %w_down.1, ...), custom_call_target="tpu_custom_call" | custom-call | tf_op jit(solution)/shard_map/pallas_call | solution.py:469
  37.9 1.1 %shard_map.85 = (bf16[8,16,8,128]{3,2,1,0:T(8,128)(2,1)}, bf16[8,2,16,2,8,128]{5,4,3,2,1,0:T(8,128)(2,1)}, f32[27,8,128]{2,1,0:T(8,128)}, f32[4,8,128]{2,1,0:T(8,128)}) custom-call(bf16[8,16,8,128]{3,2,1,0:T(8,128)(2,1)S(1)} %get-tuple-element.12.refs_0_, bf16[8,2,16,2,8,128]{5,4,3,2,1,0:T(8,128)(2,1)S(1)} %get-tuple-element.13.refs_1_, ...), custom_call_target="tpu_custom_call" | custom-call | tf_op jit(solution)/shard_map/pallas_call | solution.py:432
